TPU v7x, 512 devices: a whole 4x4x16 slice. The times are simulated.
512 devices in a mesh: rows: 128 (over y, z, core), rep: 4 (over x).
Axes of the slice: x: 4, y: 4, z: 16, core: 2. Of those that a mesh axis runs over, the one named last changes fastest.
Arguments:
- ratings: bfloat16 [8192, 128, 128], P(('rows', 'rep'))
- observed: int32 [8192, 16, 128], P(('rows', 'rep')), may hold values from 0 to 255
- user_start: bfloat16 [64, 524288], P(None, ('rows', 'rep')), may hold values from -2 to 2
- item_start: bfloat16 [64, 131072], P(None, ('rows', 'rep')), may hold values from -2 to 2
- exposure: int32 [131072], P(('rows', 'rep')), may hold values from 1 to 15
- serve_list: int32 [65536], P(('rows', 'rep')), may hold values from 0 to 2, as said below
- tile_slot: int32 [8192], P(('rows', 'rep')), may hold values from 0 to 127, as said below
- tile_user: int32 [8192], P(('rows', 'rep')), may hold values from 0 to 31
Outputs:
- user_factor: bfloat16 [64, 524288], P(None, ('rows', 'rep'))
- item_factor: bfloat16 [64, 131072], P(None, ('rows', 'rep'))
Inputs may be any that keep to these rules, and one draw needn't show every extreme that they name: serve_list holds 2 where the requesting rows index needs no block of that owner; each device needs at most one item block from each owner of its rep group, and some owner's block in every draw. `tile_slot`: every tile points to an owner whose serve_list entry for the tile's rows index is a real block.
All inputs are finite; a program needn't handle non-finite values.
Results may differ from a plain program's by a relative error of at most 0.0068.
Values may be sent and summed in bfloat16 or wider, within the bound.
A program may use at most 64 MiB of HBM per device.

v0:
```python
import math

import jax
import jax.numpy as jnp
from jax import lax
from jax.sharding import PartitionSpec as P

LEVELS = 16
ITERS = 2


def unpack_mask(packed_words):
    bit_shifts = jnp.arange(8, dtype=jnp.int32)
    bit_values = jnp.bitwise_and(jnp.right_shift(packed_words[:, :, :, None], bit_shifts), 1)
    bit_values = jnp.transpose(bit_values, (0, 2, 1, 3))
    return bit_values.reshape(
        packed_words.shape[0], packed_words.shape[2], packed_words.shape[1] * 8
    ).astype(jnp.float32)


def residual_block(rating_part, word_part, user_part, item_part, weight_part):
    predicted = jnp.einsum("gku,gki->gui", user_part, item_part, preferred_element_type=jnp.float32)
    deviation = rating_part.astype(jnp.float32) - predicted
    observed_mask = unpack_mask(word_part)
    return (observed_mask * weight_part[:, None, :].astype(jnp.float32) * deviation).astype(
        jnp.bfloat16
    )


def orthonormal(raw_factor, gram_total, row_count):
    cholesky_factor = jnp.linalg.cholesky(gram_total / row_count)
    return jax.scipy.linalg.solve_triangular(cholesky_factor, raw_factor, lower=True).astype(
        jnp.bfloat16
    )


def local_gram(raw_factor):
    return jnp.dot(raw_factor, raw_factor.T, precision=lax.Precision.HIGHEST)


def to_blocks(factor, tile_side):
    return jnp.transpose(factor.reshape(factor.shape[0], -1, tile_side), (1, 0, 2))


def from_blocks(blocks):
    return jnp.transpose(blocks, (1, 0, 2)).reshape(blocks.shape[1], -1)


def local(ratings, observed, user_start, item_start, exposure, serve_list, tile_slot, tile_user):
    tile_side = ratings.shape[2]
    factor_rank = user_start.shape[0]
    own_users = user_start.shape[1]
    peer_count = lax.axis_size("rows")
    rep_count = lax.axis_size("rep")
    user_count = own_users * peer_count * rep_count * 1.0
    item_count = item_start.shape[1] * peer_count * rep_count * 1.0
    weight = (
        ((LEVELS + 1.0) / (exposure.astype(jnp.float32) + 1.0))
        .astype(jnp.bfloat16)
        .reshape(-1, tile_side)
    )
    own_items = to_blocks(item_start, tile_side)
    block_total = own_items.shape[0]
    empty_block = jnp.zeros((1, factor_rank, tile_side), jnp.bfloat16)
    item_table = jnp.concatenate([own_items, empty_block], 0)
    weight_table = jnp.concatenate([weight, jnp.zeros((1, tile_side), jnp.bfloat16)], 0)
    fetched_items, fetched_weight = (
        lax.all_to_all(item_table[serve_list], "rows", split_axis=0, concat_axis=0, tiled=True),
        lax.all_to_all(weight_table[serve_list], "rows", split_axis=0, concat_axis=0, tiled=True),
    )
    shard_users = lax.all_gather(user_start, "rep", axis=1, tiled=True)
    user_table = to_blocks(shard_users, tile_side)
    tile_count = ratings.shape[0]
    group_size = math.gcd(tile_count, 16)
    block_count = tile_count // group_size
    tile_groups = (
        ratings.reshape(block_count, group_size, tile_side, tile_side),
        observed.reshape(block_count, group_size, observed.shape[1], tile_side),
        tile_user.reshape(block_count, group_size),
        tile_slot.reshape(block_count, group_size),
    )

    def residual_group(pieces):
        rating_part, word_part, user_idx, slot_idx = pieces
        return residual_block(
            rating_part,
            word_part,
            user_table[user_idx],
            fetched_items[slot_idx],
            fetched_weight[slot_idx],
        )

    def residual_tiles():
        return lax.map(residual_group, tile_groups).reshape(tile_count, tile_side, tile_side)

    query_items = fetched_items
    user_factor = user_start
    item_factor = item_start
    for sweep_index in range(ITERS):
        residual = residual_tiles()
        contrib = jnp.einsum(
            "tki,tui->tku", query_items[tile_slot], residual, preferred_element_type=jnp.float32
        )
        partial_value = from_blocks(
            jax.ops.segment_sum(contrib, tile_user, num_segments=user_table.shape[0])
        )
        own_part = lax.psum_scatter(partial_value, "rep", scatter_dimension=1, tiled=True)
        gram_total = lax.psum(local_gram(own_part), ("rows", "rep"))
        user_factor = orthonormal(own_part, gram_total, user_count)
        user_all = lax.all_gather(user_factor, "rep", axis=1, tiled=True)
        user_now = to_blocks(user_all, tile_side)
        residual = residual_tiles()
        back_terms = jnp.einsum(
            "tku,tui->tki", user_now[tile_user], residual, preferred_element_type=jnp.float32
        )
        slot_sums = jax.ops.segment_sum(back_terms, tile_slot, num_segments=peer_count)
        arrived = lax.all_to_all(slot_sums, "rows", split_axis=0, concat_axis=0, tiled=True)
        summed = jax.ops.segment_sum(arrived, serve_list, num_segments=block_total + 1)[:-1]
        raw_items = from_blocks(summed)
        gram_items = lax.psum(local_gram(raw_items), ("rows", "rep"))
        item_factor = orthonormal(raw_items, gram_items, item_count)
        if sweep_index + 1 < ITERS:
            next_table = jnp.concatenate([to_blocks(item_factor, tile_side), empty_block], 0)
            query_items = lax.all_to_all(
                next_table[serve_list], "rows", split_axis=0, concat_axis=0, tiled=True
            )
    return (user_factor, item_factor)


def solution(mesh):
    in_specs = (
        P(("rows", "rep"), None, None),
        P(("rows", "rep"), None, None),
        P(None, ("rows", "rep")),
        P(None, ("rows", "rep")),
        P(("rows", "rep")),
        P(("rows", "rep")),
        P(("rows", "rep")),
        P(("rows", "rep")),
    )
    out_specs = (P(None, ("rows", "rep")), P(None, ("rows", "rep")))
    return jax.shard_map(local, mesh=mesh, in_specs=in_specs, out_specs=out_specs, check_vma=False)
```

profile of v0, /device:TPU:1, one launch (start us, length us, event | category | flops | bytes accessed | tf_op | source)
XLA Modules:
  0.0 1257.9 jit_solution(14263318031003203937)
XLA Ops:
  10.0 20.6 %all-to-all-start.1 = ((bf16[128,1,128]{2,1,0:T(2,128)(2,1)}), bf16[128,1,128]{2,1,0:T(2,128)(2,1)S(1)}, u32[]{:S(2)}, u32[]{:S(2)}) async-start(bf16[128,1,128]{2,1,0:T(2,128)(2,1)} %copy.72), calls=%async_computation.1 | async-start | bytes 131072 | tf_op jit(solution)/shard_map/all_to_all | solution.py:69
  33.4 12.1 all-to-all-done.1
  45.5 7.6 all-to-all-start
  53.8 12.0 all_gather.9
  67.2 84.9 %all-to-all-done = bf16[128,64,128]{2,1,0:T(8,128)(2,1)} async-done(((bf16[128,64,128]{2,1,0:T(8,128)(2,1)}), bf16[128,64,128]{2,1,0:T(8,128)(2,1)}, u32[]{:S(2)}, u32[]{:S(2)}) %all-to-all-start) | async-done | bytes 2097184 | tf_op jit(solution)/shard_map/all_to_all | solution.py:68
  157.8 23.0 %reduce-scatter.3.cloned.1.call-done = f32[64,1024]{1,0:T(8,128)} async-done(((f32[64,4096]{1,0:T(8,128)}), f32[64,1024]{1,0:T(8,128)}) %reduce-scatter.3.cloned.1.call-update) | async-done | bytes 262160 | tf_op jit(solution)/shard_map/reduce_scatter | solution.py:107
  182.2 106.0 %psum.28 = f32[64,64]{0,1:T(8,128)S(1)} all-reduce(f32[64,64]{0,1:T(8,128)S(1)} %fusion.30), channel_id=1, replica_groups=mesh['rows'=128,'rep'=4] {'rows','rep'}, use_global_device_ids=true, to_apply=%region_2.3 | all-reduce | flops 4096 | bytes 32768 | tf_op jit(solution)/shard_map/psum | solution.py:108
  288.3 5.8 cholesky.74
  295.4 4.9 custom-call.10
  301.7 9.9 all_gather.10
  317.8 200.8 %all_to_all.32 = f32[128,64,128]{2,1,0:T(8,128)} all-to-all(f32[128,64,128]{2,1,0:T(8,128)} %scatter_fusion.1), channel_id=1, replica_groups=mesh['rows'=128,'rep'=4] {'rows'}, dimensions={0} | all-to-all | bytes 8388608 | tf_op jit(solution)/shard_map/all_to_all | solution.py:117
  518.6 13.6 %scatter_fusion.2 = f32[3,64,128]{2,1,0:T(8,128)S(1)} fusion(f32[3,64,128]{2,1,0:T(8,128)S(1)} %broadcast.119.clone, s32[128]{0:T(128)S(1)} %copy-done.6, f32[128,64,128]{2,1,0:T(8,128)} %all_to_all.32), kind=kCustom, calls=%fused_computation.11 | custom fusion | flops 1048576 | bytes 12583424 | tf_op jit(solution)/shard_map/scatter-add | solution.py:118
  532.4 102.8 %psum.29 = f32[64,64]{0,1:T(8,128)S(1)} all-reduce(f32[64,64]{0,1:T(8,128)S(1)} %convolution_bitcast_fusion.1), channel_id=1, replica_groups=mesh['rows'=128,'rep'=4] {'rows','rep'}, use_global_device_ids=true, to_apply=%region_7.10 | all-reduce | flops 4096 | bytes 32768 | tf_op jit(solution)/shard_map/psum | solution.py:120
  635.4 5.8 cholesky.85
  642.6 4.9 custom-call.11
  648.7 108.6 %all_to_all.33 = bf16[128,64,128]{2,1,0:T(8,128)(2,1)} all-to-all(bf16[128,64,128]{2,1,0:T(8,128)(2,1)S(1)} %gather_fusion.6), channel_id=1, replica_groups=mesh['rows'=128,'rep'=4] {'rows'}, dimensions={0} | all-to-all | bytes 4194304 | tf_op jit(solution)/shard_map/all_to_all | solution.py:124
  762.5 21.1 %reduce-scatter.5.cloned.1.call-done = f32[64,1024]{1,0:T(8,128)} async-done(((f32[64,4096]{1,0:T(8,128)}), f32[64,1024]{1,0:T(8,128)}) %reduce-scatter.5.cloned.1.call-update) | async-done | bytes 262160 | tf_op jit(solution)/shard_map/reduce_scatter | solution.py:107
  785.0 106.2 %psum.30 = f32[64,64]{0,1:T(8,128)S(1)} all-reduce(f32[64,64]{0,1:T(8,128)S(1)} %fusion.33), channel_id=1, replica_groups=mesh['rows'=128,'rep'=4] {'rows','rep'}, use_global_device_ids=true, to_apply=%region_10.14 | all-reduce | flops 4096 | bytes 32768 | tf_op jit(solution)/shard_map/psum | solution.py:108
  891.3 5.8 cholesky.96
  904.8 9.9 all_gather.11
  920.8 200.5 %all_to_all.34 = f32[128,64,128]{2,1,0:T(8,128)} all-to-all(f32[128,64,128]{2,1,0:T(8,128)} %scatter_fusion.4), channel_id=1, replica_groups=mesh['rows'=128,'rep'=4] {'rows'}, dimensions={0} | all-to-all | bytes 8388608 | tf_op jit(solution)/shard_map/all_to_all | solution.py:117
  1121.4 13.6 %scatter_fusion.5 = f32[3,64,128]{2,1,0:T(8,128)S(1)} fusion(f32[3,64,128]{2,1,0:T(8,128)S(1)} %broadcast.119, s32[128]{0:T(128)S(1)} %copy-done.6, f32[128,64,128]{2,1,0:T(8,128)} %all_to_all.34), kind=kCustom, calls=%fused_computation.14 | custom fusion | flops 1048576 | bytes 12583424 | tf_op jit(solution)/shard_map/scatter-add | solution.py:118
  1135.2 102.8 %psum.31 = f32[64,64]{0,1:T(8,128)S(1)} all-reduce(f32[64,64]{0,1:T(8,128)S(1)} %convolution_bitcast_fusion), channel_id=1, replica_groups=mesh['rows'=128,'rep'=4] {'rows','rep'}, use_global_device_ids=true, to_apply=%region_13.17 | all-reduce | flops 4096 | bytes 32768 | tf_op jit(solution)/shard_map/psum | solution.py:120
  1238.1 5.8 cholesky.107
  (100 shorter events, 54.3 us)
Async XLA Ops:
  7.2 46.1 %copy-start = (s32[16,16,128]{2,1,0:T(8,128)S(1)}, s32[16,16,128]{2,1,0:T(8,128)}, u32[]{:S(2)}) copy-start(s32[16,16,128]{2,1,0:T(8,128)} %param.14) | copy-start | bytes 393220
  10.0 35.5 %all-to-all-start.1 = ((bf16[128,1,128]{2,1,0:T(2,128)(2,1)}), bf16[128,1,128]{2,1,0:T(2,128)(2,1)S(1)}, u32[]{:S(2)}, u32[]{:S(2)}) async-start(bf16[128,1,128]{2,1,0:T(2,128)(2,1)} %copy.72), calls=%async_computation.1 | async-start | bytes 131072 | tf_op jit(solution)/shard_map/all_to_all | solution.py:69
  33.4 20.3 %copy-start.4 = (s32[16]{0:T(128)S(1)}, s32[16]{0:T(128)}, u32[]{:S(2)}) copy-start(s32[16]{0:T(128)} %param.20) | copy-start | bytes 196
  33.4 20.4 %copy-start.3 = (bf16[64,1024]{1,0:T(8,128)(2,1)S(1)}, bf16[64,1024]{1,0:T(8,128)(2,1)}, u32[]{:S(2)}) copy-start(bf16[64,1024]{1,0:T(8,128)(2,1)} %param.15) | copy-start | bytes 393220
  33.4 33.1 %copy-start.5 = (s32[16]{0:T(128)S(1)}, s32[16]{0:T(128)}, u32[]{:S(2)}) copy-start(s32[16]{0:T(128)} %param.19) | copy-start | bytes 196
  33.4 120.8 %copy-start.2 = (bf16[16,128,128]{2,1,0:T(8,128)(2,1)S(1)}, bf16[16,128,128]{2,1,0:T(8,128)(2,1)}, u32[]{:S(2)}) copy-start(bf16[16,128,128]{2,1,0:T(8,128)(2,1)} %param.13) | copy-start | bytes 1572868
  45.5 106.5 %all-to-all-start = ((bf16[128,64,128]{2,1,0:T(8,128)(2,1)}), bf16[128,64,128]{2,1,0:T(8,128)(2,1)}, u32[]{:S(2)}, u32[]{:S(2)}) async-start(bf16[128,64,128]{2,1,0:T(8,128)(2,1)} %gather_fusion), calls=%async_computation | async-start | bytes 4194304 | tf_op jit(solution)/shard_map/all_to_all | solution.py:68
  53.2 127.6 %reduce-scatter.3.cloned.1.call-start = ((), (), s32[]{:S(2)}) async-start(), calls=%async_computation.7 | async-start | bytes 1310720 | tf_op jit(solution)/shard_map/reduce_scatter | solution.py:107
  157.7 625.9 %reduce-scatter.5.cloned.1.call-start = ((), (), s32[]{:S(2)}) async-start(), calls=%async_computation.8 | async-start | bytes 1310720 | tf_op jit(solution)/shard_map/reduce_scatter | solution.py:107
  317.8 200.8 %copy-start.6 = (s32[128]{0:T(128)S(1)}, s32[128]{0:T(128)}, u32[]{:S(2)}) copy-start(s32[128]{0:T(128)} %param.18) | copy-start | bytes 1540
  904.8 16.1 %copy-start.1 = (bf16[64,1024]{1,0:T(8,128)(2,1)}, bf16[64,1024]{1,0:T(8,128)(2,1)S(1)}, u32[]{:S(2)}) copy-start(bf16[64,1024]{1,0:T(8,128)(2,1)S(1)} %convolution_convert_fusion) | copy-start | bytes 393220
Sparse Core Ops, SparseCore 0:
  157.9 22.8 reduce-scatter.2
  762.6 20.9 reduce-scatter.4
where the time goes:
time: 1260 us
  blocking collectives  959 us (76%)
  waiting for transfers between devices  141 us (11%)
  other arithmetic  85 us (7%)
  starting transfers between devices  28.3 us (2%)
  local copies, waits for them, and re-layouts  20.6 us (2%)
  between operations  14.5 us (1%)
    all_to_all x2, blocking collectives, local(): lax.all_to_all(slot_sums, 'rows', split_axis=0, concat_axis=0, tiled=True)  401 us
    psum x2, blocking collectives, local(): gram_total = lax.psum(local_gram(own_part), ('rows', 'rep'))  212 us
    psum x2, blocking collectives, local(): gram_items = lax.psum(local_gram(raw_items), ('rows', 'rep'))  206 us
    all_to_all x1, blocking collectives, local(): lax.all_to_all(next_table[serve_list], 'rows', split_axis=0, concat_axis=...  109 us
    all_to_all x1, waiting for transfers between devices, local(): lax.all_to_all(item_table[serve_list], 'rows', split_axis=0, concat_axis=...  84.9 us
    reduce_scatter x2, waiting for transfers between devices, local(): lax.psum_scatter(partial_value, 'rep', scatter_dimension=1, tiled=True)  44.1 us
    scatter-add x2, other arithmetic, local(): jax.ops.segment_sum(arrived, serve_list, num_segments=block_total + 1)[:-1]  27.2 us
    another operation x12, other arithmetic, orthonormal(): cholesky_factor = jnp.linalg.cholesky(gram_total / row_count)  26.1 us
  transfers between devices with their start and end apart: 4, of which 4 were waited for; matrix products, arithmetic and copies ran while one was open for 0% of the time, Pallas kernels for 0%

commit v1 on v0

v1 whole, which is shorter than its diff:
```python
import functools

import jax
import jax.numpy as jnp
from jax import lax
from jax.experimental import pallas as pl
from jax.experimental.pallas import tpu as pltpu
from jax.sharding import PartitionSpec as P

LEVELS = 16
ITERS = 2
MESH = pl.DeviceIdType.MESH
BF = jnp.bfloat16
F32 = jnp.float32
STRIP = 16
VMEM_LIMIT = 48 * 1024 * 1024


class Grid:
    def __init__(self, rows, rep):
        self.c = 2
        self.x = rep
        self.y = 4 if rows % 16 == 0 else 2
        self.z = rows // (self.c * self.y)


def place(grid):
    r = lax.axis_index("rows")
    x = lax.axis_index("rep")
    y = r // (grid.z * grid.c)
    z = (r // grid.c) % grid.z
    return x, y, z, r % grid.c


def row_of(grid, y, z, c):
    return (y * grid.z + z) * grid.c + c


def remote(src, dst, send_sem, recv_sem, r, x):
    return pltpu.make_async_remote_copy(
        src_ref=src,
        dst_ref=dst,
        send_sem=send_sem,
        recv_sem=recv_sem,
        device_id=(r, x),
        device_id_type=MESH,
    )


def greet(targets):
    barrier = pltpu.get_barrier_semaphore()
    for r, x in targets:
        pl.semaphore_signal(barrier, inc=1, device_id=(r, x), device_id_type=MESH)
    pl.semaphore_wait(barrier, len(targets))


def peers_x(grid, r, x):
    return [(r, (x + i) % grid.x) for i in range(1, grid.x)]


def peers_yc(grid, x, y, z, c):
    out = []
    for i in range(grid.y):
        for j in range(grid.c):
            if i or j:
                out.append((row_of(grid, (y + i) % grid.y, z, (c + j) % 2), x))
    return out


def peers_z(grid, x, y, z, c):
    return [(row_of(grid, y, (z + i) % grid.z, c), x) for i in range(1, grid.z)]


def plane_gather(grid, place_, buf, y_send, y_recv, z_send, z_recv, c_send, c_recv):
    x, y, z, c = place_
    half = grid.y // 2
    steps = grid.z // 2
    mine = row_of(grid, y, z, c)

    def y_copy(to, slot):
        block = buf.at[c, z, slot]
        return remote(block, block, y_send.at[to], y_recv.at[slot], row_of(grid, to, z, c), x)

    for i in range(1, grid.y):
        y_copy((y + i) % grid.y, y).start()

    def part(zz, h):
        return buf.at[c, zz, pl.ds(h * half, half)]

    def z_copy(s, h, way):
        zz = (z - s + grid.z) % grid.z if way == 0 else (z + s) % grid.z
        to = (z + 1) % grid.z if way == 0 else (z - 1 + grid.z) % grid.z
        return remote(
            part(zz, h),
            part(zz, h),
            z_send.at[way, s, h],
            z_recv.at[way, s, h],
            row_of(grid, y, to, c),
            x,
        )

    def c_copy(zz, h):
        return remote(
            part(zz, h),
            part(zz, h),
            c_send.at[zz, h],
            c_recv.at[zz, h],
            row_of(grid, y, z, 1 - c),
            x,
        )

    def c_arrival(zz, h):
        there = buf.at[1 - c, zz, pl.ds(h * half, half)]
        return remote(there, there, c_send.at[zz, h], c_recv.at[zz, h], row_of(grid, y, z, 1 - c), x)

    for i in range(1, grid.y):
        y_copy((y + i) % grid.y, (y + i) % grid.y).wait_recv()

    for h in range(2):
        for way in range(2):
            z_copy(0, h, way).start()
        c_copy(z, h).start()

    @pl.loop(1, steps)
    def _(s):
        for h in range(2):
            for way in range(2):
                z_copy(s - 1, h, way).wait_recv()
            zr = (z - s + grid.z) % grid.z
            zl = (z + s) % grid.z

            @pl.when((s < steps - 1) | (h == 0))
            def _():
                z_copy(s, h, 0).start()

            @pl.when((s < steps - 1) | (h == 1))
            def _():
                z_copy(s, h, 1).start()

            c_copy(zr, h).start()
            c_copy(zl, h).start()

    far = (z + steps) % grid.z
    last = steps - 1
    z_copy(last, 0, 0).wait_recv()
    c_copy(far, 0).start()
    z_copy(last, 1, 1).wait_recv()
    c_copy(far, 1).start()

    for i in range(1, grid.y):
        y_copy((y + i) % grid.y, y).wait_send()

    @pl.loop(0, steps)
    def _(s):
        for h in range(2):

            @pl.when((s < steps - 1) | (h == 0))
            def _():
                z_copy(s, h, 0).wait_send()

            @pl.when((s < steps - 1) | (h == 1))
            def _():
                z_copy(s, h, 1).wait_send()

    @pl.loop(0, grid.z)
    def _(zz):
        for h in range(2):
            c_copy(zz, h).wait_send()
            c_arrival(zz, h).wait_recv()


def plane_sems(grid):
    return [
        pltpu.SemaphoreType.DMA((grid.y,)),
        pltpu.SemaphoreType.DMA((grid.y,)),
        pltpu.SemaphoreType.DMA((2, grid.z // 2, 2)),
        pltpu.SemaphoreType.DMA((2, grid.z // 2, 2)),
        pltpu.SemaphoreType.DMA((grid.z, 2)),
        pltpu.SemaphoreType.DMA((grid.z, 2)),
    ]


def plane_targets(grid, x, y, z, c):
    out = [(row_of(grid, (y + i) % grid.y, z, c), x) for i in range(1, grid.y)]
    out += [(row_of(grid, y, (z + 1) % grid.z, c), x), (row_of(grid, y, (z - 1 + grid.z) % grid.z, c), x)]
    return out + [(row_of(grid, y, z, 1 - c), x)]


def x_gather(grid, place_, users, send, recv):
    x, y, z, c = place_
    r = row_of(grid, y, z, c)

    per = users.shape[0] // grid.x

    def copy(to, slot):
        block = users.at[pl.ds(slot * per, per)]
        return remote(block, block, send.at[to], recv.at[slot], r, to)

    def start():
        for i in range(1, grid.x):
            copy((x + i) % grid.x, x).start()

    def finish():
        for i in range(1, grid.x):
            copy((x + i) % grid.x, (x + i) % grid.x).wait_recv()
        for i in range(1, grid.x):
            copy((x + i) % grid.x, x).wait_send()

    return start, finish


def first_gather_kernel(grid, chunk, own_users, buf, users, x_send, x_recv, *sems):
    place_ = x, y, z, c = place(grid)
    buf[c, z, y] = chunk[...]
    users[pl.ds(x * own_users.shape[0], own_users.shape[0])] = own_users[...]
    greet(plane_targets(grid, x, y, z, c) + peers_x(grid, row_of(grid, y, z, c), x))
    start, finish = x_gather(grid, place_, users, x_send, x_recv)
    start()
    plane_gather(grid, place_, buf, *sems)
    finish()


def first_gather(grid, chunk, own_users):
    return pl.pallas_call(
        functools.partial(first_gather_kernel, grid),
        out_shape=(
            jax.ShapeDtypeStruct((2, grid.z, grid.y) + chunk.shape, BF),
            jax.ShapeDtypeStruct((grid.x * own_users.shape[0],) + own_users.shape[1:], BF),
        ),
        in_specs=[pl.BlockSpec(memory_space=pltpu.VMEM)] * 2,
        out_specs=(pl.BlockSpec(memory_space=pltpu.VMEM),) * 2,
        scratch_shapes=[pltpu.SemaphoreType.DMA((grid.x,))] * 2 + plane_sems(grid),
        compiler_params=pltpu.CompilerParams(
            collective_id=0, has_side_effects=True, vmem_limit_bytes=VMEM_LIMIT
        ),
    )(chunk, own_users)


def item_gather_kernel(grid, chunk, buf, *sems):
    place_ = x, y, z, c = place(grid)
    buf[c, z, y] = chunk[...]
    greet(plane_targets(grid, x, y, z, c))
    plane_gather(grid, place_, buf, *sems)


def item_gather(grid, chunk):
    return pl.pallas_call(
        functools.partial(item_gather_kernel, grid),
        out_shape=jax.ShapeDtypeStruct((2, grid.z, grid.y) + chunk.shape, BF),
        in_specs=[pl.BlockSpec(memory_space=pltpu.VMEM)],
        out_specs=pl.BlockSpec(memory_space=pltpu.VMEM),
        scratch_shapes=plane_sems(grid),
        compiler_params=pltpu.CompilerParams(
            collective_id=1, has_side_effects=True, vmem_limit_bytes=VMEM_LIMIT
        ),
    )(chunk)


def gram_sum(grid, place_, gram, part, first, second, third, whole, sems):
    x, y, z, c = place_
    r = row_of(grid, y, z, c)
    s1, r1, s2, r2, s3, r3, s4, r4 = sems
    k = gram.shape[0]
    rows = k // grid.x
    low = rows // 2
    for p in range(grid.x):
        part[p] = jnp.concatenate(
            [gram[p * rows : p * rows + low], gram[p * rows + low : (p + 1) * rows]], axis=1
        )

    def one(to, slot):
        return remote(part.at[to], first.at[slot], s1.at[to], r1.at[slot], r, to)

    first[x] = part[x]
    for i in range(1, grid.x):
        one((x + i) % grid.x, x).start()
    for i in range(1, grid.x):
        one((x + i) % grid.x, (x + i) % grid.x).wait_recv()
    total = first[0]
    for i in range(1, grid.x):
        total = total + first[i]

    here = y * grid.c + c
    second[here] = total

    def two(to, slot):
        return remote(
            second.at[here],
            second.at[slot],
            s2.at[to],
            r2.at[slot],
            row_of(grid, to // grid.c, z, to % grid.c),
            x,
        )

    group = grid.y * grid.c
    for i in range(1, group):
        two((here + i) % group, here).start()
    for i in range(1, group):
        two((here + i) % group, (here + i) % group).wait_recv()
    total = second[0]
    for i in range(1, group):
        total = total + second[i]

    third[z] = total

    def three(to, slot):
        return remote(third.at[z], third.at[slot], s3.at[to], r3.at[slot], row_of(grid, y, to, c), x)

    for i in range(1, grid.z):
        three((z + i) % grid.z, z).start()
    for i in range(1, grid.z):
        three((z + i) % grid.z, (z + i) % grid.z).wait_recv()
    total = third[0]
    for i in range(1, grid.z):
        total = total + third[i]

    whole[x] = total

    def four(to, slot):
        return remote(whole.at[x], whole.at[slot], s4.at[to], r4.at[slot], r, to)

    for i in range(1, grid.x):
        four((x + i) % grid.x, x).start()
    for i in range(1, grid.x):
        four((x + i) % grid.x, (x + i) % grid.x).wait_recv()
    for i in range(1, grid.x):
        one((x + i) % grid.x, x).wait_send()
        four((x + i) % grid.x, x).wait_send()
    for i in range(1, group):
        two((here + i) % group, here).wait_send()
    for i in range(1, grid.z):
        three((z + i) % grid.z, z).wait_send()
    pieces = []
    for p in range(grid.x):
        pieces += [whole[p][:, :k], whole[p][:, k:]]
    return jnp.concatenate(pieces, axis=0)


def gram_scratch(grid, rank):
    low = rank // grid.x // 2
    shape = (low, 2 * rank)
    return [
        pltpu.VMEM((grid.x,) + shape, F32),
        pltpu.VMEM((grid.x,) + shape, F32),
        pltpu.VMEM((grid.y * grid.c,) + shape, F32),
        pltpu.VMEM((grid.z,) + shape, F32),
        pltpu.VMEM((grid.x,) + shape, F32),
    ] + [
        pltpu.SemaphoreType.DMA((n,))
        for n in (grid.x, grid.x, grid.y * grid.c, grid.y * grid.c, grid.z, grid.z, grid.x, grid.x)
    ]


def block_gram(raw, blocks):
    total = None
    for i in range(blocks):
        value = raw[i]
        one = lax.dot_general(
            value,
            value,
            (((1,), (1,)), ((), ())),
            precision=lax.Precision.HIGHEST,
            preferred_element_type=F32,
        )
        total = one if total is None else total + one
    return total


def strips_at(buf, at, count):
    return jnp.concatenate([buf[at + i] for i in range(count)], axis=0)


def residual_kernel(chunk_at, pick, user_at, buf, users, ratings, observed, out, out_t, *, rank):
    side = ratings.shape[1]
    strips = rank // STRIP

    @pl.loop(0, ratings.shape[0])
    def _(t):
        b = pick[t]
        base = chunk_at[t] * (2 * strips + 1)
        items = strips_at(buf, base + b * strips, strips)
        meta = buf[base + 2 * strips].astype(F32)
        line = lax.broadcasted_iota(jnp.int32, meta.shape, 0)
        weight = jnp.sum(jnp.where(line == b, meta, 0.0), axis=0, keepdims=True)
        guess = lax.dot_general(
            users[user_at[t]], items, (((0,), (0,)), ((), ())), preferred_element_type=F32
        )
        words = observed[t]
        spread = jnp.broadcast_to(words[:, None, :], (words.shape[0], 8, side)).reshape(side, side)
        shift = lax.broadcasted_iota(jnp.int32, (side, side), 0) % 8
        mask = ((spread >> shift) & 1).astype(F32).T
        value = mask * weight * (ratings[t].astype(F32) - guess)
        out[t] = value.astype(BF)
        out_t[t] = value.T.astype(BF)


def residual_call(rank, chunk_at, pick, user_at, buf, users, ratings, observed):
    shape = jax.ShapeDtypeStruct(ratings.shape, BF)
    return pl.pallas_call(
        functools.partial(residual_kernel, rank=rank),
        out_shape=(shape, shape),
        in_specs=[pl.BlockSpec(memory_space=pltpu.SMEM)] * 3
        + [pl.BlockSpec(memory_space=pltpu.VMEM)] * 4,
        out_specs=(pl.BlockSpec(memory_space=pltpu.VMEM),) * 2,
        compiler_params=pltpu.CompilerParams(vmem_limit_bytes=VMEM_LIMIT),
    )(chunk_at, pick, user_at, buf, users, ratings, observed)


def user_half_kernel(
    grid, rank, query_at, before, last, buf, res_t, raw, gram, sums, stage, got, send, recv, *rest
):
    place_ = x, y, z, c = place(grid)
    r = row_of(grid, y, z, c)
    per = raw.shape[0]
    greet(peers_x(grid, r, x) + peers_yc(grid, x, y, z, c) + peers_z(grid, x, y, z, c))
    sums[0] = jnp.zeros_like(sums[0])

    @pl.loop(0, res_t.shape[0])
    def _(t):
        query = strips_at(buf, query_at[t], rank // STRIP)
        product = jnp.dot(query, res_t[t], preferred_element_type=F32)
        sums[t + 1] = product + sums[before[t]]

    def copy(to, slot):
        return remote(stage.at[to], got.at[slot], send.at[to], recv.at[slot], r, to)

    for i in range(1, grid.x):
        to = (x + i) % grid.x

        @pl.loop(0, per)
        def _(j):
            stage[to, j] = sums[last[to * per + j]]

        copy(to, x).start()

    @pl.loop(0, per)
    def _(j):
        raw[j] = sums[last[x * per + j]]

    for i in range(1, grid.x):
        copy((x + i) % grid.x, (x + i) % grid.x).wait_recv()

    @pl.loop(0, per)
    def _(j):
        total = raw[j]
        for i in range(1, grid.x):
            total = total + got[(x + i) % grid.x, j]
        raw[j] = total

    gram[...] = gram_sum(grid, place_, block_gram(raw, per), *rest[:5], rest[5:])
    for i in range(1, grid.x):
        copy((x + i) % grid.x, x).wait_send()


def user_half(grid, rank, per, number, tables, buf, res_t):
    side = res_t.shape[1]
    return pl.pallas_call(
        functools.partial(user_half_kernel, grid, rank),
        out_shape=(
            jax.ShapeDtypeStruct((per, rank, side), F32),
            jax.ShapeDtypeStruct((rank, rank), F32),
        ),
        in_specs=[pl.BlockSpec(memory_space=pltpu.SMEM)] * 3
        + [pl.BlockSpec(memory_space=pltpu.VMEM)] * 2,
        out_specs=(pl.BlockSpec(memory_space=pltpu.VMEM),) * 2,
        scratch_shapes=[
            pltpu.VMEM((res_t.shape[0] + 1, rank, side), F32),
            pltpu.VMEM((grid.x, per, rank, side), F32),
            pltpu.VMEM((grid.x, per, rank, side), F32),
            pltpu.SemaphoreType.DMA((grid.x,)),
            pltpu.SemaphoreType.DMA((grid.x,)),
        ]
        + gram_scratch(grid, rank),
        compiler_params=pltpu.CompilerParams(
            collective_id=number, has_side_effects=True, vmem_limit_bytes=VMEM_LIMIT
        ),
    )(*tables, buf, res_t)


def item_half_kernel(
    grid,
    user_at,
    before,
    table,
    own_users,
    res,
    raw,
    gram,
    users,
    sums,
    near,
    stage,
    got,
    x_send,
    x_recv,
    y_send,
    y_recv,
    c_send,
    c_recv,
    z_send,
    z_recv,
    *rest,
):
    place_ = x, y, z, c = place(grid)
    r = row_of(grid, y, z, c)
    tiles = res.shape[0]
    per = own_users.shape[0]
    users[pl.ds(x * per, per)] = own_users[...]
    greet(peers_x(grid, r, x) + peers_yc(grid, x, y, z, c) + peers_z(grid, x, y, z, c))
    start, finish = x_gather(grid, place_, users, x_send, x_recv)
    start()
    sums[0] = jnp.zeros_like(sums[0])
    for cc in range(grid.c):
        for yy in range(grid.y):
            near[cc, yy, 0] = jnp.zeros(near.shape[3:], BF)
    finish()

    @pl.loop(0, tiles)
    def _(t):
        product = jnp.dot(users[user_at[t]], res[t], preferred_element_type=F32)
        total = product + sums[before[t]]
        sums[t + 1] = total
        near[c, y, t + 1] = total.astype(BF)

    def y_copy(to, slot):
        block = near.at[c, slot, pl.ds(1, tiles)]
        return remote(block, block, y_send.at[to], y_recv.at[slot], row_of(grid, to, z, c), x)

    def c_copy(core, slot):
        block = near.at[core, slot, pl.ds(1, tiles)]
        return remote(block, block, c_send.at[slot], c_recv.at[slot], row_of(grid, y, z, 1 - c), x)

    for i in range(1, grid.y):
        y_copy((y + i) % grid.y, y).start()
    c_copy(c, y).start()
    for i in range(1, grid.y):
        slot = (y + i) % grid.y
        y_copy(slot, slot).wait_recv()
        c_copy(c, slot).start()
    for i in range(grid.y):
        c_copy(1 - c, (y + i) % grid.y).wait_recv()

    def z_copy(to, slot):
        return remote(stage.at[to], got.at[slot], z_send.at[to], z_recv.at[slot], row_of(grid, y, to, c), x)

    def gathered(zz, b):
        total = None
        for cc in range(grid.c):
            for yy in range(grid.y):
                at = table[((cc * grid.y + yy) * grid.z + zz) * 2 + b]
                value = near[cc, yy, at].astype(F32)
                total = value if total is None else total + value
        return total

    @pl.loop(1, grid.z)
    def _(i):
        to = (z + i) % grid.z
        for b in range(2):
            stage[to, b] = gathered(to, b).astype(BF)
        z_copy(to, z).start()

    for b in range(2):
        raw[b] = gathered(z, b)

    @pl.loop(1, grid.z)
    def _(i):
        slot = (z - i + grid.z) % grid.z
        z_copy(slot, slot).wait_recv()
        for b in range(2):
            raw[b] = raw[b] + got[slot, b].astype(F32)

    gram[...] = gram_sum(grid, place_, block_gram(raw, 2), *rest[:5], rest[5:])
    for i in range(1, grid.y):
        y_copy((y + i) % grid.y, y).wait_send()
    for i in range(grid.y):
        c_copy(c, (y + i) % grid.y).wait_send()

    @pl.loop(1, grid.z)
    def _(i):
        z_copy((z + i) % grid.z, z).wait_send()


def item_half(grid, rank, tables, own_users, res):
    tiles, side = res.shape[:2]
    return pl.pallas_call(
        functools.partial(item_half_kernel, grid),
        out_shape=(
            jax.ShapeDtypeStruct((2, rank, side), F32),
            jax.ShapeDtypeStruct((rank, rank), F32),
        ),
        in_specs=[pl.BlockSpec(memory_space=pltpu.SMEM)] * 3
        + [pl.BlockSpec(memory_space=pltpu.VMEM)] * 2,
        out_specs=(pl.BlockSpec(memory_space=pltpu.VMEM),) * 2,
        scratch_shapes=[
            pltpu.VMEM((grid.x * own_users.shape[0],) + own_users.shape[1:], BF),
            pltpu.VMEM((tiles + 1, rank, side), F32),
            pltpu.VMEM((grid.c, grid.y, tiles + 1, rank, side), BF),
            pltpu.VMEM((grid.z, 2, rank, side), BF),
            pltpu.VMEM((grid.z, 2, rank, side), BF),
        ]
        + [
            pltpu.SemaphoreType.DMA((n,))
            for n in (grid.x, grid.x, grid.y, grid.y, grid.y, grid.y, grid.z, grid.z)
        ]
        + gram_scratch(grid, rank),
        compiler_params=pltpu.CompilerParams(
            collective_id=3, has_side_effects=True, vmem_limit_bytes=VMEM_LIMIT
        ),
    )(*tables, own_users, res)


def orthonormal(raw_blocks, gram_total, row_count):
    rank = gram_total.shape[0]
    factor = jnp.linalg.cholesky(gram_total / row_count)
    raw = jnp.transpose(raw_blocks, (1, 0, 2)).reshape(rank, -1)
    return jax.scipy.linalg.solve_triangular(factor, raw, lower=True).astype(BF)


def to_blocks(factor, side):
    return jnp.transpose(factor.reshape(factor.shape[0], -1, side), (1, 0, 2))


def links(ids):
    n = ids.shape[0]
    at = jnp.arange(n, dtype=jnp.int32)
    same = (ids[:, None] == ids[None, :]) & (at[None, :] < at[:, None])
    return jnp.max(jnp.where(same, at[None, :] + 1, 0), axis=1)


def local(grid, ratings, observed, user_start, item_start, exposure, serve_list, tile_slot, tile_user):
    side = ratings.shape[2]
    rank, own_users = user_start.shape
    tiles = ratings.shape[0]
    owners = grid.y * grid.z * grid.c
    user_count = own_users * owners * grid.x * 1.0
    item_count = item_start.shape[1] * owners * grid.x * 1.0
    per = own_users // side
    x, y, z, c = place(grid)

    weight = ((LEVELS + 1.0) / (exposure.astype(F32) + 1.0)).astype(BF).reshape(2, side)
    meta = jnp.zeros((16, side), BF)
    meta = meta.at[0:2].set(weight)
    meta = meta.at[2, :owners].set(serve_list.astype(BF))
    meta = meta.at[3, :tiles].set(tile_slot.astype(BF))
    chunk = jnp.concatenate([to_blocks(item_start, side).reshape(-1, STRIP, side), meta[None]], 0)
    buf, users = first_gather(grid, chunk, to_blocks(user_start, side))

    notes = buf[:, :, :, 2 * rank // STRIP, 2:4, :].astype(jnp.int32)
    group = lax.dynamic_index_in_dim(notes, z, 1, keepdims=False)[:, :, 1, :tiles]
    slots = group.reshape(grid.c * grid.y, tiles)
    serves = notes[:, :, :, 0, :owners].reshape(owners, grid.y, grid.z, grid.c)
    serves = lax.dynamic_index_in_dim(serves, z, 2, keepdims=False)
    serves = jnp.transpose(serves, (2, 1, 0)).reshape(grid.c * grid.y, owners)
    sy = slots // (grid.z * grid.c)
    sz = (slots // grid.c) % grid.z
    sc = slots % grid.c
    where = (sc * grid.z + sz) * grid.y + sy
    hit = where[:, :, None] == jnp.arange(owners, dtype=jnp.int32)
    picks = jnp.sum(jnp.where(hit, serves[:, None, :], 0), axis=2)
    own = c * grid.y + y
    chunk_at = lax.dynamic_index_in_dim(where, own, 0, keepdims=False)
    pick = lax.dynamic_index_in_dim(picks, own, 0, keepdims=False)
    before_item = links(chunk_at * 2 + pick)
    place_of = jnp.where((sy == y) & (sc == c), sz * 2 + picks, -1)
    table = jnp.max(
        jnp.where(
            place_of[:, None, :] == jnp.arange(2 * grid.z, dtype=jnp.int32)[None, :, None],
            jnp.arange(1, tiles + 1, dtype=jnp.int32),
            0,
        ),
        axis=2,
    ).reshape(-1)
    before_user = links(tile_user)
    last_user = jnp.max(
        jnp.where(
            tile_user[None, :] == jnp.arange(grid.x * per, dtype=jnp.int32)[:, None],
            jnp.arange(1, tiles + 1, dtype=jnp.int32),
            0,
        ),
        axis=1,
    )

    strips = rank // STRIP
    flat = buf.reshape(-1, STRIP, side)
    query_at = chunk_at * (2 * strips + 1) + pick * strips
    res, res_t = residual_call(
        rank, chunk_at, pick, tile_user, flat, users, ratings, observed
    )
    query = flat
    for sweep in range(ITERS):
        raw_user, gram_user = user_half(
            grid, rank, per, 2 if sweep == 0 else 4, (query_at, before_user, last_user), query, res_t
        )
        user_factor = orthonormal(raw_user, gram_user, user_count)
        raw_item, gram_item = item_half(
            grid, rank, (tile_user, before_item, table), to_blocks(user_factor, side), res
        )
        item_factor = orthonormal(raw_item, gram_item, item_count)
        if sweep + 1 < ITERS:
            chunk = to_blocks(item_factor, side).reshape(-1, STRIP, side)
            query = item_gather(grid, chunk).reshape(-1, STRIP, side)
            query_at = (chunk_at * 2 + pick) * strips
    return user_factor, item_factor


def solution(mesh):
    grid = Grid(mesh.shape["rows"], mesh.shape["rep"])
    both = P(("rows", "rep"))
    second = P(None, ("rows", "rep"))
    return jax.shard_map(
        functools.partial(local, grid),
        mesh=mesh,
        in_specs=(both, both, second, second, both, both, both, both),
        out_specs=(second, second),
        check_vma=False,
    )
```

time: 1260 us -> 411 us (0.33)
  blocking collectives: 959 us -> 0 us
  Pallas kernels: 0 us -> 346 us
  waiting for transfers between devices: 141 us -> 0 us
  other arithmetic: 85 us -> 51.3 us
  starting transfers between devices: 28.3 us -> 0 us
  between operations: 14.5 us -> 1.11 us
    all_to_all x3 -> x0, blocking collectives: 510 us -> none  [the longest x2 401 us: local(): lax.all_to_all(slot_sums, 'rows', split_axis=0, concat_axis=0, tiled=True)]
    psum x4 -> x0, blocking collectives: 418 us -> none  [the longest x2 212 us: local(): gram_total = lax.psum(local_gram(own_part), ('rows', 'rep'))]
    pallas_call x0 -> x7, Pallas kernels: none -> 346 us  [the longest x2 158 us: item_half(): pl.pallas_call(functools.partial(item_half_kernel, grid), out_shape=(jax....]
    all_to_all x2 -> x0, waiting for transfers between devices: 97 us -> none  [the longest x1 84.9 us: local(): lax.all_to_all(item_table[serve_list], 'rows', split_axis=0, concat_axis=...]
    reduce_scatter x2 -> x0, waiting for transfers between devices: 44.1 us -> none  [local(): lax.psum_scatter(partial_value, 'rep', scatter_dimension=1, tiled=True)]
    scatter-add x6 -> x0, other arithmetic: 35.2 us -> none  [the longest x2 27.2 us: local(): jax.ops.segment_sum(arrived, serve_list, num_segments=block_total + 1)[:-1]]
    all_gather x3 -> x0, blocking collectives: 31.8 us -> none  [the longest x2 19.8 us: local(): user_all = lax.all_gather(user_factor, 'rep', axis=1, tiled=True)]
    all_to_all x2 -> x0, starting transfers between devices: 28.2 us -> none  [the longest x1 20.6 us: local(): lax.all_to_all(weight_table[serve_list], 'rows', split_axis=0, concat_axi...]
  transfers between devices with their start and end apart: 4 -> 0, of which waited for: 4 -> 0; matrix products, arithmetic and copies ran while one was open for 0% -> 0% of each run, Pallas kernels for 0% -> 0%
where the time goes in v1:
time: 411 us; the launch traced here: 410 us
  Pallas kernels  346 us (84%)
  other arithmetic  51.3 us (12%)
  local copies, waits for them, and re-layouts  10.2 us (2%)
    pallas_call x2, Pallas kernels, item_half(): pl.pallas_call(functools.partial(item_half_kernel, grid), out_shape=(jax....  158 us
    pallas_call x2, Pallas kernels, user_half(): pl.pallas_call(functools.partial(user_half_kernel, grid, rank), out_shape...  82.9 us
    pallas_call x1, Pallas kernels, first_gather(): pl.pallas_call(functools.partial(first_gather_kernel, grid), out_shape=(j...  54 us
    pallas_call x1, Pallas kernels, item_gather(): pl.pallas_call(functools.partial(item_gather_kernel, grid), out_shape=jax...  44.2 us
    another operation x12, other arithmetic, orthonormal(): factor = jnp.linalg.cholesky(gram_total / row_count)  26.1 us
    another operation x8, other arithmetic, orthonormal(): return jax.scipy.linalg.solve_triangular(factor, raw, lower=True).astype(BF)  22.2 us

profile of v1, /device:TPU:1, one launch (start us, length us, event | category | flops | bytes accessed | tf_op | source)
XLA Modules:
  0.0 410.3 jit_solution(9912680676652753633)
XLA Ops:
  0.7 0.8 fusion.34
  1.5 0.7 convert_bitcast_fusion.1
  2.2 0.7 convert_bitcast_fusion
  3.0 0.8 copy_bitcast_fusion.1
  3.9 54.0 %shard_map.95 = (bf16[2,16,4,9,16,128]{5,4,3,2,1,0:T(8,128)(2,1)S(1)}, bf16[32,64,128]{2,1,0:T(8,128)(2,1)S(1)}) custom-call(bf16[9,16,128]{2,1,0:T(8,128)(2,1)S(1)} %pad_maximum_fusion.chunk, bf16[8,64,128]{2,1,0:T(8,128)(2,1)S(1)} %bitcast_bitcast_fusion.2.own_users), custom_call_target="tpu_custom_call" | custom-call | tf_op jit(solution)/shard_map/pallas_call | solution.py:224
  57.9 2.1 copy-done.1
  60.2 2.9 copy.59
  63.1 3.3 reshape_squeeze.7
  67.4 6.9 %shard_map.96 = (bf16[16,128,128]{2,1,0:T(8,128)(2,1)S(1)}, bf16[16,128,128]{2,1,0:T(8,128)(2,1)S(1)}) custom-call(s32[16]{0:T(128)S(1)} %get-tuple-element.68.chunk_at, s32[16]{0:T(128)S(1)} %get-tuple-element.69.pick, s32[16]{0:T(128)S(1)} %copy-done.5, bf16[1152,16,128]{2,1,0:T(8,128)(2,1)} %bitcast.138, ...), custom_call_target="tpu_custom_call" | custom-call | tf_op jit(solution)/shard_map/pallas_call | solution.py:400
  74.3 40.8 %shard_map.97 = (f32[8,64,128]{2,1,0:T(8,128)S(1)}, f32[64,64]{1,0:T(8,128)S(1)}) custom-call(s32[16]{0:T(128)S(1)} %get-tuple-element.67.query_at, s32[16]{0:T(128)S(1)} %get-tuple-element.66.before, s32[32]{0:T(128)S(1)} %select_reduce_fusion.5.last, bf16[1152,16,128]{2,1,0:T(8,128)(2,1)S(1)} %bitcast.139, bf16[16,128,128]{2,1,0:T(8,128)(2,1)S(1)} %get-tuple-element.55.res_t), custom_call_target="tpu_custom_call" | custom-call | tf_op jit(solution)/shard_map/pallas_call | solution.py:458
  115.3 5.8 %cholesky.74 = f32[64,64]{1,0:T(8,128)S(1)} custom-call(f32[64,64]{1,0:T(8,128)S(1)} %fusion.21), custom_call_target="Cholesky" | custom-call | tf_op jit(solution)/shard_map/jit(cholesky)/cholesky | solution.py:615
  122.5 4.9 %custom-call.10 = f32[1,64,64]{1,2,0:T(8,128)S(1)} custom-call(f32[1,64,64]{2,1,0:T(8,128)S(1)} %fusion.10), custom_call_target="InvertDiagBlocksLowerTriangular" | custom-call | tf_op jit(solution)/shard_map/jit(_solve_triangular)/triangular_solve | solution.py:617
  127.8 78.5 %shard_map.98 = (f32[2,64,128]{2,1,0:T(8,128)S(1)}, f32[64,64]{1,0:T(8,128)S(1)}) custom-call(s32[16]{0:T(128)S(1)} %copy-done.5, s32[16]{0:T(128)S(1)} %get-tuple-element.65.before, s32[256]{0:T(256)S(1)} %reshape.317.table, bf16[8,64,128]{2,1,0:T(8,128)(2,1)S(1)} %bitcast.141, bf16[16,128,128]{2,1,0:T(8,128)(2,1)S(1)} %get-tuple-element.58.res), custom_call_target="tpu_custom_call" | custom-call | tf_op jit(solution)/shard_map/pallas_call | solution.py:586
  206.5 5.8 %cholesky.85 = f32[64,64]{1,0:T(8,128)S(1)} custom-call(f32[64,64]{1,0:T(8,128)S(1)} %fusion.19), custom_call_target="Cholesky" | custom-call | tf_op jit(solution)/shard_map/jit(cholesky)/cholesky | solution.py:615
  213.0 0.7 fusion.11
  213.7 4.9 %custom-call.11 = f32[1,64,64]{1,2,0:T(8,128)S(1)} custom-call(f32[1,64,64]{2,1,0:T(8,128)S(1)} %fusion.11), custom_call_target="InvertDiagBlocksLowerTriangular" | custom-call | tf_op jit(solution)/shard_map/jit(_solve_triangular)/triangular_solve | solution.py:617
  218.9 44.2 %shard_map.99 = bf16[2,16,4,8,16,128]{5,4,3,2,1,0:T(8,128)(2,1)S(1)} custom-call(bf16[8,16,128]{2,1,0:T(8,128)(2,1)S(1)} %bitcast.142), custom_call_target="tpu_custom_call" | custom-call | tf_op jit(solution)/shard_map/pallas_call | solution.py:247
  263.1 42.1 %shard_map.100 = (f32[8,64,128]{2,1,0:T(8,128)S(1)}, f32[64,64]{1,0:T(8,128)S(1)}) custom-call(s32[16]{0:T(128)S(1)} %get-tuple-element.70.query_at, s32[16]{0:T(128)S(1)} %get-tuple-element.66.before, s32[32]{0:T(128)S(1)} %select_reduce_fusion.5.last, bf16[1024,16,128]{2,1,0:T(8,128)(2,1)S(1)} %bitcast.140, bf16[16,128,128]{2,1,0:T(8,128)(2,1)S(1)} %get-tuple-element.55.res_t), custom_call_target="tpu_custom_call" | custom-call | tf_op jit(solution)/shard_map/pallas_call | solution.py:458
  305.4 5.8 %cholesky.96 = f32[64,64]{1,0:T(8,128)S(1)} custom-call(f32[64,64]{1,0:T(8,128)S(1)} %fusion.17), custom_call_target="Cholesky" | custom-call | tf_op jit(solution)/shard_map/jit(cholesky)/cholesky | solution.py:615
  312.6 4.9 %custom-call.12 = f32[1,64,64]{1,2,0:T(8,128)S(1)} custom-call(f32[1,64,64]{2,1,0:T(8,128)S(1)} %fusion.12), custom_call_target="InvertDiagBlocksLowerTriangular" | custom-call | tf_op jit(solution)/shard_map/jit(_solve_triangular)/triangular_solve | solution.py:617
  318.0 79.2 %shard_map.101 = (f32[2,64,128]{2,1,0:T(8,128)S(1)}, f32[64,64]{1,0:T(8,128)S(1)}) custom-call(s32[16]{0:T(128)S(1)} %copy-done.5, s32[16]{0:T(128)S(1)} %get-tuple-element.65.before, s32[256]{0:T(256)S(1)} %reshape.317.table, bf16[8,64,128]{2,1,0:T(8,128)(2,1)S(1)} %bitcast_bitcast_fusion.own_users, bf16[16,128,128]{2,1,0:T(8,128)(2,1)S(1)} %get-tuple-element.58.res), custom_call_target="tpu_custom_call" | custom-call | tf_op jit(solution)/shard_map/pallas_call | solution.py:586
  397.4 5.8 %cholesky.107 = f32[64,64]{1,0:T(8,128)S(1)} custom-call(f32[64,64]{1,0:T(8,128)S(1)} %fusion.15), custom_call_target="Cholesky" | custom-call | tf_op jit(solution)/shard_map/jit(cholesky)/cholesky | solution.py:615
  404.6 4.9 %custom-call.13 = f32[1,64,64]{1,2,0:T(8,128)S(1)} custom-call(f32[1,64,64]{2,1,0:T(8,128)S(1)} %fusion.13), custom_call_target="InvertDiagBlocksLowerTriangular" | custom-call | tf_op jit(solution)/shard_map/jit(_solve_triangular)/triangular_solve | solution.py:617
  409.5 0.9 convolution_convert_fusion.2
  (67 shorter events, 7.8 us)
Async XLA Ops:
  0.6 3.2 copy-start
  0.6 66.4 %copy-start.5 = (s32[16]{0:T(128)S(1)}, s32[16]{0:T(128)}, u32[]{:S(2)}) copy-start(s32[16]{0:T(128)} %user_at.5) | copy-start | bytes 196
  0.7 66.7 %copy-start.4 = (s32[16,16,128]{2,1,0:T(8,128)S(1)}, s32[16,16,128]{2,1,0:T(8,128)}, u32[]{:S(2)}) copy-start(s32[16,16,128]{2,1,0:T(8,128)} %observed.1) | copy-start | bytes 393220
  0.7 66.7 %copy-start.3 = (bf16[16,128,128]{2,1,0:T(8,128)(2,1)S(1)}, bf16[16,128,128]{2,1,0:T(8,128)(2,1)}, u32[]{:S(2)}) copy-start(bf16[16,128,128]{2,1,0:T(8,128)(2,1)} %ratings.1) | copy-start | bytes 1572868
  57.9 2.1 copy-start.1
  67.1 7.2 %copy-start.2 = (bf16[2,16,4,9,16,128]{5,4,3,2,1,0:T(8,128)(2,1)S(1)}, bf16[2,16,4,9,16,128]{5,4,3,2,1,0:T(8,128)(2,1)}, u32[]{:S(2)}) copy-start(bf16[2,16,4,9,16,128]{5,4,3,2,1,0:T(8,128)(2,1)} %copy-done.1) | copy-start | bytes 14155780
  317.9 92.4 %copy-start.6 = (bf16[64,1024]{1,0:T(8,128)(2,1)}, bf16[64,1024]{1,0:T(8,128)(2,1)S(1)}, u32[]{:S(2)}) copy-start(bf16[64,1024]{1,0:T(8,128)(2,1)S(1)} %convolution_convert_fusion) | copy-start | bytes 393220

commit v2 on v0

v2 whole, which is shorter than its diff:
```python
import functools

import jax
import jax.numpy as jnp
from jax import lax
from jax.experimental import pallas as pl
from jax.experimental.pallas import tpu as pltpu
from jax.sharding import PartitionSpec as P

LEVELS = 16
ITERS = 2
MESH = pl.DeviceIdType.MESH
BF = jnp.bfloat16
F32 = jnp.float32
HIGHEST = lax.Precision.HIGHEST
VMEM_LIMIT = 48 * 1024 * 1024


class Grid:
    def __init__(self, rows, rep):
        self.c = 2
        self.x = rep
        self.y = 4
        self.z = rows // (self.c * self.y)


class Here:
    def __init__(self, grid):
        r = lax.axis_index("rows")
        self.grid = grid
        self.r = r
        self.x = lax.axis_index("rep")
        self.y = r // (grid.z * grid.c)
        self.z = (r // grid.c) % grid.z
        self.c = r % grid.c

    def along_x(self, to):
        return self.r, to

    def along_y(self, to):
        return (to * self.grid.z + self.z) * self.grid.c + self.c, self.x

    def along_z(self, to):
        return (self.y * self.grid.z + to) * self.grid.c + self.c, self.x

    def along_yc(self, to):
        y, c = to // self.grid.c, to % self.grid.c
        return (y * self.grid.z + self.z) * self.grid.c + c, self.x

    def other_core(self):
        return (self.y * self.grid.z + self.z) * self.grid.c + 1 - self.c, self.x

    def z_off(self, by):
        return (self.z + by + 2 * self.grid.z) % self.grid.z

    def far_z(self):
        return [4 * k for k in range(1, self.grid.z // 4)]

    def greet(self):
        grid = self.grid
        targets = [self.along_x((self.x + i) % grid.x) for i in range(1, grid.x)]
        for i in range(grid.y):
            for j in range(grid.c):
                if i or j:
                    to = ((self.y + i) % grid.y) * grid.c + (self.c + j) % 2
                    targets.append(self.along_yc(to))
        offsets = {o % grid.z for o in [1, 2, 3, -1, -2, -3] + self.far_z()} - {0}
        targets += [self.along_z(self.z_off(o)) for o in sorted(offsets)]
        barrier = pltpu.get_barrier_semaphore()
        for target in targets:
            pl.semaphore_signal(barrier, inc=1, device_id=target, device_id_type=MESH)
        pl.semaphore_wait(barrier, len(targets))


def remote(src, dst, send_sem, recv_sem, device):
    return pltpu.make_async_remote_copy(
        src_ref=src,
        dst_ref=dst,
        send_sem=send_sem,
        recv_sem=recv_sem,
        device_id=device,
        device_id_type=MESH,
    )


def sems(*shape):
    return pltpu.SemaphoreType.DMA(shape)


def spread_x(here, buf, per, send, recv):
    n = here.grid.x

    def copy(to, slot):
        block = buf.at[pl.ds(slot * per, per)]
        return remote(block, block, send.at[to], recv.at[slot], here.along_x(to))

    for i in range(1, n):
        copy((here.x + i) % n, here.x).start()
    yield
    for i in range(1, n):
        copy((here.x + i) % n, (here.x + i) % n).wait_recv()
    yield
    for i in range(1, n):
        copy((here.x + i) % n, here.x).wait_send()
    yield


def spread_z_sems(grid):
    far = grid.z // 4
    return [sems(far), sems(far), sems(far, 4), sems(far, 4), sems(1), sems(1)]


def spread_z(here, buf, n, far_send, far_recv, near_send, near_recv, c_send, c_recv):
    grid = here.grid
    half = n // 2
    far = grid.z // 4

    def chunk(core, zz, start=0, count=n):
        return buf.at[pl.ds((core * grid.z + zz) * n + start, count)]

    def far_copy(k):
        block = chunk(here.c, here.z)
        return remote(block, block, far_send.at[k], far_recv.at[k], here.along_z(here.z_off(4 * k)))

    def far_arrival(k):
        block = chunk(here.c, here.z_off(-4 * k))
        return remote(block, block, far_send.at[k], far_recv.at[k], here.along_z(here.z_off(-4 * k)))

    ways = [(1, 0, n), (-1, 0, n), (-2, 0, half), (2, half, half)]

    def near_copy(k, way):
        by, start, count = ways[way]
        block = chunk(here.c, here.z_off(-4 * k), start, count)
        return remote(
            block, block, near_send.at[k, way], near_recv.at[k, way], here.along_z(here.z_off(by))
        )

    def near_arrival(k, way):
        by, start, count = ways[way]
        block = chunk(here.c, here.z_off(-by - 4 * k), start, count)
        return remote(
            block, block, near_send.at[k, way], near_recv.at[k, way], here.along_z(here.z_off(-by))
        )

    for k in range(1, far):
        far_copy(k).start()
    for way in range(4):
        near_copy(0, way).start()
    yield
    for k in range(1, far):
        far_arrival(k).wait_recv()
        for way in range(4):
            near_copy(k, way).start()
    yield
    for k in range(far):
        for way in range(4):
            near_arrival(k, way).wait_recv()
    line = buf.at[pl.ds(here.c * grid.z * n, grid.z * n)]
    swap = remote(line, line, c_send.at[0], c_recv.at[0], here.other_core())
    swap.start()
    yield
    line = buf.at[pl.ds((1 - here.c) * grid.z * n, grid.z * n)]
    remote(line, line, c_send.at[0], c_recv.at[0], here.other_core()).wait_recv()
    yield
    swap.wait_send()
    for k in range(far):
        if k:
            far_copy(k).wait_send()
        for way in range(4):
            near_copy(k, way).wait_send()
    yield


def exchange(n, me, device, put, take, send, recv):
    def copy(to):
        return remote(put(to), take(me), send.at[to], recv.at[me], device(to))

    def arrival(slot):
        return remote(put(slot), take(slot), send.at[slot], recv.at[slot], device(slot))

    for i in range(1, n):
        copy((me + i) % n).start()
    yield
    for i in range(1, n):
        arrival((me + i) % n).wait_recv()
    yield
    for i in range(1, n):
        copy((me + i) % n).wait_send()
    yield


def add_up(ref, n):
    total = ref[0]
    for i in range(1, n):
        total = total + ref[i]
    return total


def gram_scratch(grid, rank):
    shape = (rank // grid.x // 2, 2 * rank)
    counts = [grid.x, grid.y * grid.c, 4, grid.z // 4, grid.x]
    buffers = [pltpu.VMEM((n,) + shape, F32) for n in [grid.x] + counts]
    return buffers + [sems(n) for n in counts for _ in range(2)] + [pltpu.VMEM((rank, 2 * rank), F32)]


def gram_steps(here, raw, blocks, row_count, scratch):
    grid = here.grid
    part, first, second, third, fourth, whole = scratch[:6]
    pairs = [scratch[6 + 2 * i : 8 + 2 * i] for i in range(5)]
    work = scratch[-1]
    total = None
    for i in range(blocks):
        value = raw[i]
        one = lax.dot_general(
            value, value, (((1,), (1,)), ((), ())), precision=HIGHEST, preferred_element_type=F32
        )
        total = one if total is None else total + one
    k = total.shape[0]
    rows = k // grid.x
    low = rows // 2
    for p in range(grid.x):
        part[p] = jnp.concatenate(
            [total[p * rows : p * rows + low], total[p * rows + low : (p + 1) * rows]], axis=1
        )
    x, z = here.x, here.z
    group = here.y * grid.c + here.c
    level, across = z // 4, z % 4
    first[x] = part[x]
    ends = []

    def run(n, me, device, put, ref, pair):
        steps = exchange(n, me, device, put, lambda slot: ref.at[slot], *pair)
        next(steps)
        ends.append(steps)
        return steps

    steps = run(grid.x, x, here.along_x, lambda to: part.at[to], first, pairs[0])
    yield
    next(steps)
    second[group] = add_up(first, grid.x)
    mine = second.at[group]
    steps = run(grid.y * grid.c, group, here.along_yc, lambda to: mine, second, pairs[1])
    yield
    next(steps)
    third[across] = add_up(second, grid.y * grid.c)
    mine = third.at[across]
    steps = run(4, across, lambda to: here.along_z(level * 4 + to), lambda to: mine, third, pairs[2])
    yield
    next(steps)
    fourth[level] = add_up(third, 4)
    mine = fourth.at[level]
    steps = run(
        grid.z // 4, level, lambda to: here.along_z(to * 4 + across), lambda to: mine, fourth, pairs[3]
    )
    yield
    next(steps)
    whole[x] = add_up(fourth, grid.z // 4)
    mine = whole.at[x]
    steps = run(grid.x, x, here.along_x, lambda to: mine, whole, pairs[4])
    yield
    next(steps)
    row = lax.broadcasted_iota(jnp.int32, (low, k), 0)
    lane = lax.broadcasted_iota(jnp.int32, (low, k), 1)
    for p in range(grid.x):
        for h in range(2):
            at = p * rows + h * low
            unit = jnp.where(row + at == lane, 1.0, 0.0).astype(F32)
            value = whole[p][:, h * k : (h + 1) * k] * (1.0 / row_count)
            work[at : at + low, :] = jnp.concatenate([value, unit], axis=1)
    for steps in ends:
        next(steps)
    yield
    row = lax.broadcasted_iota(jnp.int32, (k, 2 * k), 0)
    lane = lax.broadcasted_iota(jnp.int32, (k, 2 * k), 1)

    @pl.loop(0, k)
    def _(i):
        value = work[...]
        pivot_row = work[pl.ds(i, 1), :]
        pivot = jnp.sum(jnp.where(lane[:1] == i, pivot_row, 0.0), axis=1, keepdims=True)
        column = jnp.sum(jnp.where(lane == i, value, 0.0), axis=1, keepdims=True)
        factor = jnp.where(row[:, :1] > i, column * (1.0 / pivot), 0.0)
        work[...] = value - factor * pivot_row

    value = work[...]
    diagonal = jnp.sum(jnp.where(lane == row, value, 0.0), axis=1, keepdims=True)
    work[...] = value * lax.rsqrt(diagonal)
    yield


def apply_inverse(work, value):
    k = work.shape[0]
    return jnp.dot(work[:, k:], value, precision=HIGHEST, preferred_element_type=F32)


def first_kernel(grid, chunk, note, own_users, line, notes, users, x_send, x_recv, y_send, y_recv, *rest):
    here = Here(grid)
    per = own_users.shape[0]
    n = chunk.shape[0]
    line[pl.ds((here.c * grid.z + here.z) * n, n)] = chunk[...]
    base = (here.c * grid.z + here.z) * grid.y
    notes[base + here.y] = note[...]
    users[pl.ds(here.x * per, per)] = own_users[...]
    here.greet()
    mine = notes.at[base + here.y]
    note_y = exchange(
        grid.y, here.y, here.along_y, lambda to: mine, lambda slot: notes.at[base + slot], y_send, y_recv
    )
    next(note_y)
    items = spread_z(here, line, n, *rest[:6])
    next(items)
    people = spread_x(here, users, per, x_send, x_recv)
    next(people)
    next(note_y)
    note_z = spread_z(here, notes, grid.y, *rest[6:])
    next(note_z)
    next(items)
    next(note_z)
    next(items)
    next(note_z)
    for steps in (items, note_z, people):
        next(steps)
    for steps in (items, note_z, people, note_y):
        next(steps)


def first_gather(grid, chunk, note, own_users):
    lines = 2 * grid.z
    return pl.pallas_call(
        functools.partial(first_kernel, grid),
        out_shape=(
            jax.ShapeDtypeStruct((lines * chunk.shape[0],) + chunk.shape[1:], BF),
            jax.ShapeDtypeStruct((lines * grid.y,) + note.shape, BF),
            jax.ShapeDtypeStruct((grid.x * own_users.shape[0],) + own_users.shape[1:], BF),
        ),
        in_specs=[pl.BlockSpec(memory_space=pltpu.VMEM)] * 3,
        out_specs=(pl.BlockSpec(memory_space=pltpu.VMEM),) * 3,
        scratch_shapes=[sems(grid.x)] * 2 + [sems(grid.y)] * 2 + spread_z_sems(grid) * 2,
        compiler_params=pltpu.CompilerParams(
            collective_id=0, has_side_effects=True, vmem_limit_bytes=VMEM_LIMIT
        ),
    )(chunk, note, own_users)


def residual_tiles(tables, query, notes, users, ratings, observed, out, out_t):
    tiles, side = ratings.shape[:2]

    @pl.loop(0, tiles)
    def _(t):
        meta = notes[tables["note_at"][t]].astype(F32)
        line = lax.broadcasted_iota(jnp.int32, meta.shape, 0)
        weight = jnp.sum(jnp.where(line == tables["pick"][t], meta, 0.0), axis=0, keepdims=True)
        guess = lax.dot_general(
            users[tables["user_at"][t]],
            query[tables["query_at"][t]],
            (((0,), (0,)), ((), ())),
            preferred_element_type=F32,
        )
        words = observed[t]
        spread = jnp.broadcast_to(words[:, None, :], (words.shape[0], 8, side)).reshape(side, side)
        shift = lax.broadcasted_iota(jnp.int32, (side, side), 0) % 8
        mask = ((spread >> shift) & 1).astype(F32).T
        value = mask * weight * (ratings[t].astype(F32) - guess)
        out[t] = value.astype(BF)
        out_t[t] = value.T.astype(BF)


TABLES = ("user_at", "query_at", "note_at", "pick", "ask", "user_before", "user_last", "item_before", "item_table")


def main_kernel(grid, counts, names, *refs):
    refs = list(refs)
    tables = {name: refs.pop(0) for name in TABLES}
    line, notes, users, ratings, observed, user_out, item_out = (refs.pop(0) for _ in range(7))
    scratch = {name: refs.pop(0) for name in names}
    here = Here(grid)
    tiles, side = ratings.shape[:2]
    per = user_out.shape[1] // side
    rank = user_out.shape[0]
    x, y, z, c = here.x, here.y, here.z, here.c
    res, res_t, sums = scratch["res"], scratch["res_t"], scratch["sums"]
    near_rows = tiles + 1
    far = grid.z // 4

    def of(prefix, it):
        start = f"{prefix}{it}_"
        return [ref for name, ref in scratch.items() if name.startswith(start)]

    here.greet()
    sums[0] = jnp.zeros_like(sums[0])
    for it in range(ITERS):
        near = scratch[f"near{it}"]
        for s in range(grid.c * grid.y):
            near[s * near_rows] = jnp.zeros(near.shape[1:], BF)
    ends = []
    gram_item = None
    for it in range(ITERS):
        sel, query, stage_x, got_x, raw_u, new_users, near, stage, got, fars, got_far, raw_i = (
            scratch[f"{name}{it}"]
            for name in (
                "sel",
                "query",
                "stage_x",
                "got_x",
                "raw_u",
                "users",
                "near",
                "stage",
                "got",
                "fars",
                "got_far",
                "raw_i",
            )
        )
        for i in range(grid.y):
            to = (y + i) % grid.y

            @pl.loop(0, tiles)
            def _(t):
                sel[to * tiles + t] = line[tables["ask"][to * tiles + t]]

        asked = exchange(
            grid.y,
            y,
            here.along_y,
            lambda to: sel.at[pl.ds(to * tiles, tiles)],
            lambda slot: query.at[pl.ds(slot * tiles, tiles)],
            *of("ysel", it),
        )
        next(asked)
        query[pl.ds(y * tiles, tiles)] = sel[pl.ds(y * tiles, tiles)]
        if gram_item is not None:
            next(gram_item)
        next(asked)
        ends.append(asked)
        if it == 0:
            residual_tiles(tables, query, notes, users, ratings, observed, res, res_t)

        @pl.loop(0, tiles)
        def _(t):
            product = jnp.dot(query[tables["query_at"][t]], res_t[t], preferred_element_type=F32)
            sums[t + 1] = product + sums[tables["user_before"][t]]

        for i in range(grid.x):
            to = (x + i) % grid.x

            @pl.loop(0, per)
            def _(j):
                stage_x[to * per + j] = sums[tables["user_last"][to * per + j]]

        parts = exchange(
            grid.x,
            x,
            here.along_x,
            lambda to: stage_x.at[pl.ds(to * per, per)],
            lambda slot: got_x.at[pl.ds(slot * per, per)],
            *of("xsum", it),
        )
        next(parts)
        if gram_item is not None:
            for _ in range(3):
                next(gram_item)
        next(parts)
        ends.append(parts)

        @pl.loop(0, per)
        def _(j):
            total = stage_x[x * per + j]
            for i in range(1, grid.x):
                total = total + got_x[((x + i) % grid.x) * per + j]
            if it:
                total = apply_inverse(scratch[f"gitem{it - 1}_work"], total)
            raw_u[j] = total
            new_users[x * per + j] = total.astype(BF)

        people = spread_x(here, new_users, per, *of("xall", it))
        next(people)
        gram_user = gram_steps(here, raw_u, per, counts[0], of("guser", it))
        next(gram_user)
        next(people)
        next(gram_user)
        ends.append(people)

        @pl.loop(0, tiles)
        def _(t):
            product = jnp.dot(new_users[tables["user_at"][t]], res[t], preferred_element_type=F32)
            total = product + sums[tables["item_before"][t]]
            sums[t + 1] = total
            near[(c * grid.y + y) * near_rows + 1 + t] = total.astype(BF)

        def rows_of(core, slot):
            return near.at[pl.ds((core * grid.y + slot) * near_rows + 1, tiles)]

        along = exchange(
            grid.y, y, here.along_y, lambda to: rows_of(c, y), lambda slot: rows_of(c, slot), *of("ynear", it)
        )
        next(along)
        c_send, c_recv = of("cnear", it)

        def c_copy(core, slot):
            block = rows_of(core, slot)
            return remote(block, block, c_send.at[slot], c_recv.at[slot], here.other_core())

        c_copy(c, y).start()
        next(gram_user)
        next(along)
        ends.append(along)
        for i in range(1, grid.y):
            c_copy(c, (y + i) % grid.y).start()
        next(gram_user)
        for i in range(grid.y):
            c_copy(1 - c, (y + i) % grid.y).wait_recv()

        def gathered(zz, b):
            total = None
            for s in range(grid.c * grid.y):
                at = tables["item_table"][(s * grid.z + zz) * 2 + b]
                value = near[at].astype(F32)
                total = value if total is None else total + value
            return total

        z_send, z_recv = of("znear", it)
        ways = [(1, (0, 1)), (-1, (0, 1)), (-2, (0,)), (2, (1,))]
        starts = [0, 2 * far, 4 * far, 5 * far]

        def near_z(way, arrival=False):
            by, parts_ = ways[way]
            count = len(parts_) * far
            to = here.along_z(here.z_off(-by if arrival else by))
            return remote(
                stage.at[pl.ds(starts[way], count)],
                got.at[pl.ds(starts[way], count)],
                z_send.at[way],
                z_recv.at[way],
                to,
            )

        for way, (by, parts_) in enumerate(ways):

            @pl.loop(0, far)
            def _(k):
                for j, b in enumerate(parts_):
                    zz = here.z_off(by + 4 * k)
                    stage[starts[way] + len(parts_) * k + j] = gathered(zz, b).astype(BF)

            near_z(way).start()
        next(gram_user)
        for k in range(far):
            for b in range(2):
                fars[2 * k + b] = gathered(here.z_off(4 * k), b)
        next(gram_user)
        for way in range(4):
            near_z(way, True).wait_recv()
        f_send, f_recv = of("zfar", it)
        far_stage = scratch[f"far_stage{it}"]

        def far_copy(k):
            return remote(
                far_stage.at[pl.ds(2 * k, 2)],
                got_far.at[pl.ds(2 * k, 2)],
                f_send.at[k],
                f_recv.at[k],
                here.along_z(here.z_off(4 * k)),
            )

        for k in list(range(1, far)) + [0]:
            for b in range(2):
                total = (
                    fars[2 * k + b]
                    + got[starts[0] + 2 * k + b].astype(F32)
                    + got[starts[1] + 2 * k + b].astype(F32)
                    + got[starts[2 + b] + k].astype(F32)
                )
                if k:
                    far_stage[2 * k + b] = total.astype(BF)
                else:
                    raw_i[b] = total
            if k:
                far_copy(k).start()
        next(gram_user)
        for k in range(1, far):
            far_copy(k).wait_recv()
        for b in range(2):
            total = raw_i[b]
            for k in range(1, far):
                total = total + got_far[2 * k + b].astype(F32)
            raw_i[b] = apply_inverse(scratch[f"guser{it}_work"], total)
        gram_item = gram_steps(here, raw_i, 2, counts[1], of("gitem", it))
        if it + 1 < ITERS:
            line = scratch["line"]
            for b in range(2):
                line[(c * grid.z + z) * 2 + b] = raw_i[b].astype(BF)
            items = spread_z(here, line, 2, *of("zall", it))
            next(items)
            next(gram_item)
            next(items)
            next(gram_item)
            next(items)
            next(gram_item)
            next(items)
            ends.append(items)
        else:
            next(gram_item)
            for j in range(per):
                user_out[:, j * side : (j + 1) * side] = apply_inverse(
                    scratch[f"guser{it}_work"], raw_u[j]
                ).astype(BF)
            for _ in range(6):
                next(gram_item)
            for b in range(2):
                item_out[:, b * side : (b + 1) * side] = apply_inverse(
                    scratch[f"gitem{it}_work"], raw_i[b]
                ).astype(BF)
        for i in range(grid.y):
            c_copy(c, (y + i) % grid.y).wait_send()
        for way in range(4):
            near_z(way).wait_send()
        for k in range(1, far):
            far_copy(k).wait_send()
    for steps in ends:
        next(steps)


def main_scratch(grid, rank, side, tiles, per):
    far = grid.z // 4
    block = (rank, side)

    def vmem(n, kind=BF):
        return pltpu.VMEM((n,) + block, kind)

    out = {
        "res": pltpu.VMEM((tiles, side, side), BF),
        "res_t": pltpu.VMEM((tiles, side, side), BF),
        "sums": vmem(tiles + 1, F32),
        "line": vmem(2 * grid.z * 2),
    }
    for it in range(ITERS):
        out[f"sel{it}"] = vmem(grid.y * tiles)
        out[f"query{it}"] = vmem(grid.y * tiles)
        out[f"stage_x{it}"] = vmem(grid.x * per, F32)
        out[f"got_x{it}"] = vmem(grid.x * per, F32)
        out[f"raw_u{it}"] = vmem(per, F32)
        out[f"users{it}"] = vmem(grid.x * per)
        out[f"near{it}"] = vmem(grid.c * grid.y * (tiles + 1))
        out[f"stage{it}"] = vmem(6 * far)
        out[f"got{it}"] = vmem(6 * far)
        out[f"fars{it}"] = vmem(2 * far, F32)
        out[f"far_stage{it}"] = vmem(2 * far)
        out[f"got_far{it}"] = vmem(2 * far)
        out[f"raw_i{it}"] = vmem(2, F32)
        for name, n in (
            ("ysel", grid.y),
            ("xsum", grid.x),
            ("xall", grid.x),
            ("ynear", grid.y),
            ("cnear", grid.y),
            ("znear", 4),
            ("zfar", far),
        ):
            out[f"{name}{it}_send"] = sems(n)
            out[f"{name}{it}_recv"] = sems(n)
        for i, shape in enumerate(spread_z_sems(grid)):
            out[f"zall{it}_{i}"] = shape
        for name in ("guser", "gitem"):
            shapes = gram_scratch(grid, rank)
            for i, shape in enumerate(shapes):
                out[f"{name}{it}_" + ("work" if i + 1 == len(shapes) else str(i))] = shape
    return out


def main_call(grid, counts, tables, line, notes, users, ratings, observed):
    tiles, side = ratings.shape[:2]
    rank = line.shape[1]
    per = users.shape[0] // grid.x
    scratch = main_scratch(grid, rank, side, tiles, per)
    return pl.pallas_call(
        functools.partial(main_kernel, grid, counts, tuple(scratch)),
        out_shape=(
            jax.ShapeDtypeStruct((rank, per * side), BF),
            jax.ShapeDtypeStruct((rank, 2 * side), BF),
        ),
        in_specs=[pl.BlockSpec(memory_space=pltpu.SMEM)] * len(TABLES)
        + [pl.BlockSpec(memory_space=pltpu.VMEM)] * 5,
        out_specs=(pl.BlockSpec(memory_space=pltpu.VMEM),) * 2,
        scratch_shapes=list(scratch.values()),
        compiler_params=pltpu.CompilerParams(
            collective_id=1, has_side_effects=True, vmem_limit_bytes=VMEM_LIMIT
        ),
    )(*(tables[name] for name in TABLES), line, notes, users, ratings, observed)


def to_blocks(factor, side):
    return jnp.transpose(factor.reshape(factor.shape[0], -1, side), (1, 0, 2))


def links(ids):
    at = jnp.arange(ids.shape[0], dtype=jnp.int32)
    same = (ids[:, None] == ids[None, :]) & (at[None, :] < at[:, None])
    return jnp.max(jnp.where(same, at[None, :] + 1, 0), axis=1)


def lasts(ids, n):
    tiles = ids.shape[-1]
    same = ids[..., None, :] == jnp.arange(n, dtype=jnp.int32)[:, None]
    return jnp.max(jnp.where(same, jnp.arange(1, tiles + 1, dtype=jnp.int32), 0), axis=-1)


def local(grid, ratings, observed, user_start, item_start, exposure, serve_list, tile_slot, tile_user):
    side = ratings.shape[2]
    own_users = user_start.shape[1]
    tiles = ratings.shape[0]
    owners = grid.y * grid.z * grid.c
    counts = (own_users * owners * grid.x * 1.0, item_start.shape[1] * owners * grid.x * 1.0)
    per = own_users // side
    r = lax.axis_index("rows")
    y, z, c = r // (grid.z * grid.c), (r // grid.c) % grid.z, r % grid.c

    weight = ((LEVELS + 1.0) / (exposure.astype(F32) + 1.0)).astype(BF).reshape(2, side)
    serve = jnp.zeros((1, side), BF).at[0, :owners].set(serve_list.astype(BF))
    slot = jnp.zeros((1, side), BF).at[0, :tiles].set(tile_slot.astype(BF))
    note = jnp.concatenate([weight, serve, slot, jnp.zeros((12, side), BF)], 0)
    line, notes, users = first_gather(grid, to_blocks(item_start, side), note, to_blocks(user_start, side))

    known = notes.reshape(grid.c, grid.z, grid.y, 16, side)[:, :, :, 2:4].astype(jnp.int32)
    slots = lax.dynamic_index_in_dim(known, z, 1, keepdims=False)[:, :, 1, :tiles]
    slots = slots.reshape(grid.c * grid.y, tiles)
    serves = known[:, :, :, 0, :owners].reshape(owners, grid.y, grid.z, grid.c)
    serves = lax.dynamic_index_in_dim(serves, z, 2, keepdims=False)
    serves = jnp.transpose(serves, (2, 1, 0)).reshape(grid.c * grid.y, owners)
    sy, sz, sc = slots // (grid.z * grid.c), (slots // grid.c) % grid.z, slots % grid.c
    where = (sc * grid.z + sz) * grid.y + sy
    hit = where[:, :, None] == jnp.arange(owners, dtype=jnp.int32)
    picks = jnp.sum(jnp.where(hit, serves[:, None, :], 0), axis=2)
    in_line = (sc * grid.z + sz) * 2 + picks
    asks = jnp.where(sy == y, in_line, 0).reshape(grid.c, grid.y, tiles)
    own = c * grid.y + y

    def mine(value):
        return lax.dynamic_index_in_dim(value, own, 0, keepdims=False)

    note_at, pick = mine(where), mine(picks)
    last = lasts(jnp.where((sy == y) & (sc == c), sz * 2 + picks, -1), 2 * grid.z)
    first_row = jnp.arange(grid.c * grid.y, dtype=jnp.int32)[:, None] * (tiles + 1)
    tables = {
        "user_at": tile_user,
        "query_at": mine(sy) * tiles + jnp.arange(tiles, dtype=jnp.int32),
        "note_at": note_at,
        "pick": pick,
        "ask": lax.dynamic_index_in_dim(asks, c, 0, keepdims=False).reshape(-1),
        "user_before": links(tile_user),
        "user_last": lasts(tile_user, grid.x * per),
        "item_before": links(note_at * 2 + pick),
        "item_table": (last + first_row).reshape(-1),
    }
    return main_call(grid, counts, tables, line, notes, users, ratings, observed)


def solution(mesh):
    grid = Grid(mesh.shape["rows"], mesh.shape["rep"])
    both = P(("rows", "rep"))
    second = P(None, ("rows", "rep"))
    return jax.shard_map(
        functools.partial(local, grid),
        mesh=mesh,
        in_specs=(both, both, second, second, both, both, both, both),
        out_specs=(second, second),
        check_vma=False,
    )
```

time: 1260 us -> 277 us (0.22)
  blocking collectives: 959 us -> 0 us
  Pallas kernels: 0 us -> 253 us
  waiting for transfers between devices: 141 us -> 0 us
  other arithmetic: 85 us -> 6.47 us
  starting transfers between devices: 28.3 us -> 0 us
  between operations: 14.5 us -> 0.89 us
    all_to_all x3 -> x0, blocking collectives: 510 us -> none  [the longest x2 401 us: local(): lax.all_to_all(slot_sums, 'rows', split_axis=0, concat_axis=0, tiled=True)]
    psum x4 -> x0, blocking collectives: 418 us -> none  [the longest x2 212 us: local(): gram_total = lax.psum(local_gram(own_part), ('rows', 'rep'))]
    pallas_call x0 -> x2, Pallas kernels: none -> 253 us  [the longest x1 216 us: main_call(): pl.pallas_call(functools.partial(main_kernel, grid, counts, tuple(scratch...]
    all_to_all x2 -> x0, waiting for transfers between devices: 97 us -> none  [the longest x1 84.9 us: local(): lax.all_to_all(item_table[serve_list], 'rows', split_axis=0, concat_axis=...]
    another operation x20 -> x2, other arithmetic: 48.3 us -> 1.94 us  [the longest x12 26.1 us: orthonormal(): cholesky_factor = jnp.linalg.cholesky(gram_total / row_count)]
    reduce_scatter x2 -> x0, waiting for transfers between devices: 44.1 us -> none  [local(): lax.psum_scatter(partial_value, 'rep', scatter_dimension=1, tiled=True)]
    scatter-add x6 -> x0, other arithmetic: 35.2 us -> none  [the longest x2 27.2 us: local(): jax.ops.segment_sum(arrived, serve_list, num_segments=block_total + 1)[:-1]]
    all_gather x3 -> x0, blocking collectives: 31.8 us -> none  [the longest x2 19.8 us: local(): user_all = lax.all_gather(user_factor, 'rep', axis=1, tiled=True)]
  transfers between devices with their start and end apart: 4 -> 0, of which waited for: 4 -> 0; matrix products, arithmetic and copies ran while one was open for 0% -> 0% of each run, Pallas kernels for 0% -> 0%
where the time goes in v2:
time: 277 us; the launch traced here: 275 us
  Pallas kernels  253 us (91%)
  local copies, waits for them, and re-layouts  14.5 us (5%)
  other arithmetic  6.47 us (2%)
    pallas_call x1, Pallas kernels, main_call(): pl.pallas_call(functools.partial(main_kernel, grid, counts, tuple(scratch...  216 us
    pallas_call x1, Pallas kernels, first_gather(): pl.pallas_call(functools.partial(first_kernel, grid), out_shape=(jax.Shap...  37.4 us
    unnamed x13, local copies, waits for them, and re-layouts  6.6 us

profile of v2, /device:TPU:1, one launch (start us, length us, event | category | flops | bytes accessed | tf_op | source)
XLA Modules:
  0.0 275.3 jit_solution(5541044346960963812)
XLA Ops:
  0.7 0.9 copy-done
  1.6 0.8 bitcast_bitcast_fusion.1.chunk
  2.3 0.6 compare_reduce_fusion
  3.0 1.3 fusion.24
  4.3 0.1 pad.10.clone
  4.4 0.7 convert_bitcast_fusion
  5.0 0.7 fusion.28
  5.8 37.4 %shard_map.95 = (bf16[64,64,128]{2,1,0:T(8,128)(2,1)S(1)}, bf16[128,16,128]{2,1,0:T(8,128)(2,1)S(1)}, bf16[32,64,128]{2,1,0:T(8,128)(2,1)S(1)}) custom-call(bf16[2,64,128]{2,1,0:T(8,128)(2,1)S(1)} %bitcast_bitcast_fusion.1.chunk, bf16[16,128]{1,0:T(8,128)(2,1)S(1)} %fusion.8.note, bf16[8,64,128]{2,1,0:T(8,128)(2,1)S(1)} %bitcast_bitcast_fusion.own_users), custom_call_target="tpu_custom_call" | custom-call | tf_op jit(solution)/shard_map/pallas_call | solution.py:329
  43.3 2.5 copy.25
  45.8 2.2 convert_element_type.19
  48.0 1.9 copy-done.4
  49.9 0.3 constant_dynamic-slice_fusion.16
  50.2 0.1 copy.23
  50.4 3.1 %slice.44 = s32[2,16,4,1,128]{2,1,0,4,3:T(8,128)} slice(s32[2,16,4,2,128]{2,1,0,4,3:T(8,128)} %copy-done.4), slice={[0:2], [0:16], [0:4], [0:1], [0:128]} | slice | bytes 131072 | tf_op jit(solution)/shard_map/slice | solution.py:727
  53.5 3.3 %reshape_squeeze.9 = s32[128,4,16,2]{0,3,2,1:T(2,128)S(1)} reshape(s32[2,16,4,1,128]{2,1,0,4,3:T(8,128)} %slice.44) | data formatting | bytes 131072 | tf_op jit(solution)/shard_map/reshape;squeeze | solution.py:727
  56.9 0.3 select_reduce_fusion.1
  57.2 0.2 select_reduce_fusion.2
  57.5 0.1 reshape.261.refs_4_
  57.6 0.1 select_reduce_fusion
  57.8 0.1 add.186.refs_8_
  57.9 0.1 select_reduce_fusion.3.refs_6_
  58.0 216.0 %shard_map.96 = (bf16[64,1024]{1,0:T(8,128)(2,1)S(1)}, bf16[64,256]{1,0:T(8,128)(2,1)S(1)}) custom-call(s32[16]{0:T(128)S(1)} %copy-done.3, s32[16]{0:T(128)S(1)} %get-tuple-element.49.refs_1_, s32[16]{0:T(128)S(1)} %get-tuple-element.36.refs_2_, s32[16]{0:T(128)S(1)} %get-tuple-element.35.refs_3_, s32[64]{0:T(128)S(1)} %reshape.261.refs_4_, ...), custom_call_target="tpu_custom_call" | custom-call | tf_op jit(solution)/shard_map/pallas_call | solution.py:676
  274.0 0.7 copy.32
  274.7 0.6 copy.33
  (26 shorter events, 0.4 us)
Async XLA Ops:
  0.6 0.9 copy-start
  48.0 1.9 copy-start.4
  49.9 7.3 %copy-start.3 = (s32[16]{0:T(128)S(1)}, s32[16]{0:T(128)}, u32[]{:S(2)}) copy-start(s32[16]{0:T(128)} %refs_0_.1) | copy-start | bytes 196
  49.9 8.0 %copy-start.1 = (bf16[16,128,128]{2,1,0:T(8,128)(2,1)S(1)}, bf16[16,128,128]{2,1,0:T(8,128)(2,1)}, u32[]{:S(2)}) copy-start(bf16[16,128,128]{2,1,0:T(8,128)(2,1)} %refs_12_.1) | copy-start | bytes 1572868
  49.9 8.0 %copy-start.2 = (s32[16,16,128]{2,1,0:T(8,128)S(1)}, s32[16,16,128]{2,1,0:T(8,128)}, u32[]{:S(2)}) copy-start(s32[16,16,128]{2,1,0:T(8,128)} %refs_13_.1) | copy-start | bytes 393220

commit v3 on v2

--- a/solution.py
+++ b/solution.py
@@ -53,9 +53,6 @@
     def z_off(self, by):
         return (self.z + by + 2 * self.grid.z) % self.grid.z
 
-    def far_z(self):
-        return [4 * k for k in range(1, self.grid.z // 4)]
-
     def greet(self):
         grid = self.grid
         targets = [self.along_x((self.x + i) % grid.x) for i in range(1, grid.x)]
@@ -64,8 +61,7 @@
                 if i or j:
                     to = ((self.y + i) % grid.y) * grid.c + (self.c + j) % 2
                     targets.append(self.along_yc(to))
-        offsets = {o % grid.z for o in [1, 2, 3, -1, -2, -3] + self.far_z()} - {0}
-        targets += [self.along_z(self.z_off(o)) for o in sorted(offsets)]
+        targets += [self.along_z(self.z_off(o)) for o in range(1, grid.z)]
         barrier = pltpu.get_barrier_semaphore()
         for target in targets:
             pl.semaphore_signal(barrier, inc=1, device_id=target, device_id_type=MESH)
@@ -198,15 +194,15 @@
 
 def gram_scratch(grid, rank):
     shape = (rank // grid.x // 2, 2 * rank)
-    counts = [grid.x, grid.y * grid.c, 4, grid.z // 4, grid.x]
+    counts = [grid.x, grid.y * grid.c, grid.z, grid.x]
     buffers = [pltpu.VMEM((n,) + shape, F32) for n in [grid.x] + counts]
     return buffers + [sems(n) for n in counts for _ in range(2)] + [pltpu.VMEM((rank, 2 * rank), F32)]
 
 
 def gram_steps(here, raw, blocks, row_count, scratch):
     grid = here.grid
-    part, first, second, third, fourth, whole = scratch[:6]
-    pairs = [scratch[6 + 2 * i : 8 + 2 * i] for i in range(5)]
+    part, first, second, third, whole = scratch[:5]
+    pairs = [scratch[5 + 2 * i : 7 + 2 * i] for i in range(4)]
     work = scratch[-1]
     total = None
     for i in range(blocks):
@@ -224,7 +220,6 @@
         )
     x, z = here.x, here.z
     group = here.y * grid.c + here.c
-    level, across = z // 4, z % 4
     first[x] = part[x]
     ends = []
 
@@ -239,24 +234,17 @@
     next(steps)
     second[group] = add_up(first, grid.x)
     mine = second.at[group]
-    steps = run(grid.y * grid.c, group, here.along_yc, lambda to: mine, second, pairs[1])
+    steps = run(grid.y * grid.c, group, here.along_yc, lambda to, mine=mine: mine, second, pairs[1])
     yield
     next(steps)
-    third[across] = add_up(second, grid.y * grid.c)
-    mine = third.at[across]
-    steps = run(4, across, lambda to: here.along_z(level * 4 + to), lambda to: mine, third, pairs[2])
+    third[z] = add_up(second, grid.y * grid.c)
+    mine = third.at[z]
+    steps = run(grid.z, z, here.along_z, lambda to, mine=mine: mine, third, pairs[2])
     yield
     next(steps)
-    fourth[level] = add_up(third, 4)
-    mine = fourth.at[level]
-    steps = run(
-        grid.z // 4, level, lambda to: here.along_z(to * 4 + across), lambda to: mine, fourth, pairs[3]
-    )
-    yield
-    next(steps)
-    whole[x] = add_up(fourth, grid.z // 4)
+    whole[x] = add_up(third, grid.z)
     mine = whole.at[x]
-    steps = run(grid.x, x, here.along_x, lambda to: mine, whole, pairs[4])
+    steps = run(grid.x, x, here.along_x, lambda to, mine=mine: mine, whole, pairs[3])
     yield
     next(steps)
     row = lax.broadcasted_iota(jnp.int32, (low, k), 0)
@@ -273,14 +261,24 @@
     row = lax.broadcasted_iota(jnp.int32, (k, 2 * k), 0)
     lane = lax.broadcasted_iota(jnp.int32, (k, 2 * k), 1)
 
-    @pl.loop(0, k)
+    def lane_sum(value, at):
+        return jnp.sum(jnp.where(lane[: value.shape[0]] == at, value, 0.0), axis=1, keepdims=True)
+
+    @pl.loop(0, k // 2)
     def _(i):
+        at = 2 * i
         value = work[...]
-        pivot_row = work[pl.ds(i, 1), :]
-        pivot = jnp.sum(jnp.where(lane[:1] == i, pivot_row, 0.0), axis=1, keepdims=True)
-        column = jnp.sum(jnp.where(lane == i, value, 0.0), axis=1, keepdims=True)
-        factor = jnp.where(row[:, :1] > i, column * (1.0 / pivot), 0.0)
-        work[...] = value - factor * pivot_row
+        upper = work[pl.ds(at, 1), :]
+        lower = work[pl.ds(at + 1, 1), :]
+        inverse = 1.0 / lane_sum(upper, at)
+        cross = lane_sum(upper, at + 1)
+        left = lane_sum(value, at) * inverse
+        lower = lower - (cross * inverse) * upper
+        right = lane_sum(value, at + 1) - left * cross
+        right = right * (1.0 / (lane_sum(lower, at + 1)))
+        left = jnp.where(row[:, :1] > at, left, 0.0)
+        right = jnp.where(row[:, :1] > at + 1, right, 0.0)
+        work[...] = value - left * upper - right * lower
 
     value = work[...]
     diagonal = jnp.sum(jnp.where(lane == row, value, 0.0), axis=1, keepdims=True)
@@ -293,85 +291,101 @@
     return jnp.dot(work[:, k:], value, precision=HIGHEST, preferred_element_type=F32)
 
 
-def first_kernel(grid, chunk, note, own_users, line, notes, users, x_send, x_recv, y_send, y_recv, *rest):
-    here = Here(grid)
-    per = own_users.shape[0]
-    n = chunk.shape[0]
-    line[pl.ds((here.c * grid.z + here.z) * n, n)] = chunk[...]
-    base = (here.c * grid.z + here.z) * grid.y
-    notes[base + here.y] = note[...]
-    users[pl.ds(here.x * per, per)] = own_users[...]
-    here.greet()
-    mine = notes.at[base + here.y]
-    note_y = exchange(
-        grid.y, here.y, here.along_y, lambda to: mine, lambda slot: notes.at[base + slot], y_send, y_recv
+def slots_of(grid, value):
+    return value // (grid.z * grid.c), (value // grid.c) % grid.z, value % grid.c
+
+
+def work_out_tables(here, tiles, notes, serves, column_table, item_table):
+    grid = here.grid
+    group = grid.c * grid.y
+    n = group * tiles
+    owners = grid.c * grid.z * grid.y
+    side = notes.shape[2]
+
+    @pl.loop(0, owners)
+    def _(i):
+        serves[pl.ds(i, 1), :] = notes[i][2:3].astype(F32)
+
+    row = lax.broadcasted_iota(jnp.int32, (n, side), 0)
+    lane = lax.broadcasted_iota(jnp.int32, (n, side), 1)
+    tile, member = row % tiles, row // tiles
+    asked = []
+    for core in range(grid.c):
+        for y in range(grid.y):
+            line = notes[(core * grid.z + here.z) * grid.y + y][3:4].astype(F32)
+            asked.append(jnp.broadcast_to(line, (tiles, side)))
+    asked = jnp.concatenate(asked, axis=0)
+
+    def column(value):
+        return jnp.sum(value, axis=1, keepdims=True)
+
+    slot = column(jnp.where(lane == tile, asked, 0.0)).astype(jnp.int32)
+    sy, sz, sc = slots_of(grid, slot)
+    where = (sc * grid.z + sz) * grid.y + sy
+    hot = jnp.where(lane == where, 1.0, 0.0).astype(BF)[:, :owners]
+    served = jnp.dot(hot, serves[...].astype(BF), preferred_element_type=F32)
+    asker = ((member % grid.y) * grid.z + here.z) * grid.c + member // grid.y
+    pick = column(jnp.where(lane == asker, served, 0.0)).astype(jnp.int32)
+    line_at = (sc * grid.z + sz) * 2 + pick
+    ask = jnp.where(sy == here.y, line_at, 0)
+    ids = where * 2 + pick
+    across = jnp.broadcast_to(ids.astype(F32), (n, side)).T.astype(jnp.int32)[:n]
+    square_lane, square_row = lane[:, :n], row[:, :n]
+    same = (across == ids) & (square_lane // tiles == square_row // tiles) & (square_lane < square_row)
+    before = jnp.max(jnp.where(same, square_lane % tiles + 1, 0).astype(F32), axis=1, keepdims=True)
+    columns = jnp.where(
+        lane == 0, ask.astype(F32), jnp.where(lane == 1, pick.astype(F32), jnp.where(lane == 2, before, 0.0))
     )
-    next(note_y)
-    items = spread_z(here, line, n, *rest[:6])
-    next(items)
-    people = spread_x(here, users, per, x_send, x_recv)
-    next(people)
-    next(note_y)
-    note_z = spread_z(here, notes, grid.y, *rest[6:])
-    next(note_z)
-    next(items)
-    next(note_z)
-    next(items)
-    next(note_z)
-    for steps in (items, note_z, people):
-        next(steps)
-    for steps in (items, note_z, people, note_y):
-        next(steps)
-
-
-def first_gather(grid, chunk, note, own_users):
-    lines = 2 * grid.z
-    return pl.pallas_call(
-        functools.partial(first_kernel, grid),
-        out_shape=(
-            jax.ShapeDtypeStruct((lines * chunk.shape[0],) + chunk.shape[1:], BF),
-            jax.ShapeDtypeStruct((lines * grid.y,) + note.shape, BF),
-            jax.ShapeDtypeStruct((grid.x * own_users.shape[0],) + own_users.shape[1:], BF),
-        ),
-        in_specs=[pl.BlockSpec(memory_space=pltpu.VMEM)] * 3,
-        out_specs=(pl.BlockSpec(memory_space=pltpu.VMEM),) * 3,
-        scratch_shapes=[sems(grid.x)] * 2 + [sems(grid.y)] * 2 + spread_z_sems(grid) * 2,
-        compiler_params=pltpu.CompilerParams(
-            collective_id=0, has_side_effects=True, vmem_limit_bytes=VMEM_LIMIT
-        ),
-    )(chunk, note, own_users)
-
-
-def residual_tiles(tables, query, notes, users, ratings, observed, out, out_t):
-    tiles, side = ratings.shape[:2]
-
-    @pl.loop(0, tiles)
+    column_table[...] = columns.T[:8].astype(jnp.int32)
+    mine = jnp.where((sy == here.y) & (sc == here.c), sz * 2 + pick, -1)
+    number = jnp.where(mine == lane, tile + 1, 0).astype(F32)
+    for g in range(group):
+        last = jnp.max(number[g * tiles : (g + 1) * tiles], axis=0, keepdims=True)
+        item_table[g : g + 1, :] = last.astype(jnp.int32) + g * (tiles + 1)
+
+
+def within(at, ref):
+    return jnp.minimum(jnp.maximum(at, 0), ref.shape[0] - 1)
+
+
+def unpack_masks(observed, masks):
+    side = masks.shape[1]
+
+    @pl.loop(0, masks.shape[0])
+    def _(t):
+        words = observed[t]
+        spread = jnp.broadcast_to(words[:, None, :], (words.shape[0], 8, side)).reshape(side, side)
+        shift = lax.broadcasted_iota(jnp.int32, (side, side), 0) % 8
+        masks[t] = ((spread >> shift) & 1).astype(F32).T.astype(BF)
+
+
+def residual_tiles(tables, own, query, notes, users, ratings, masks, out, out_t):
+    tiles = ratings.shape[0]
+
+    @pl.loop(0, tiles, unroll=4)
     def _(t):
         meta = notes[tables["note_at"][t]].astype(F32)
         line = lax.broadcasted_iota(jnp.int32, meta.shape, 0)
-        weight = jnp.sum(jnp.where(line == tables["pick"][t], meta, 0.0), axis=0, keepdims=True)
+        pick = tables["column"][1, own * tiles + t]
+        weight = jnp.sum(jnp.where(line == pick, meta, 0.0), axis=0, keepdims=True)
         guess = lax.dot_general(
             users[tables["user_at"][t]],
             query[tables["query_at"][t]],
             (((0,), (0,)), ((), ())),
             preferred_element_type=F32,
         )
-        words = observed[t]
-        spread = jnp.broadcast_to(words[:, None, :], (words.shape[0], 8, side)).reshape(side, side)
-        shift = lax.broadcasted_iota(jnp.int32, (side, side), 0) % 8
-        mask = ((spread >> shift) & 1).astype(F32).T
-        value = mask * weight * (ratings[t].astype(F32) - guess)
+        value = masks[t].astype(F32) * weight * (ratings[t].astype(F32) - guess)
         out[t] = value.astype(BF)
         out_t[t] = value.T.astype(BF)
 
 
-TABLES = ("user_at", "query_at", "note_at", "pick", "ask", "user_before", "user_last", "item_before", "item_table")
+TABLES = ("user_at", "query_at", "note_at", "user_before", "user_last")
 
 
 def main_kernel(grid, counts, names, *refs):
     refs = list(refs)
     tables = {name: refs.pop(0) for name in TABLES}
-    line, notes, users, ratings, observed, user_out, item_out = (refs.pop(0) for _ in range(7))
+    facts, item_start, user_start, ratings, observed, user_out, item_out = (refs.pop(0) for _ in range(7))
     scratch = {name: refs.pop(0) for name in names}
     here = Here(grid)
     tiles, side = ratings.shape[:2]
@@ -386,13 +400,62 @@
         start = f"{prefix}{it}_"
         return [ref for name, ref in scratch.items() if name.startswith(start)]
 
+    line, notes, users = scratch["line"], scratch["notes"], scratch["users"]
+    ends = []
+
+    for b in range(2):
+        line[(c * grid.z + z) * 2 + b] = item_start[:, b * side : (b + 1) * side]
+    for j in range(per):
+        users[x * per + j] = user_start[:, j * side : (j + 1) * side]
+    facts_f = facts[...].astype(F32)
+    weight = (LEVELS + 1.0) / (facts_f + 1.0)
+    facts_row = lax.broadcasted_iota(jnp.int32, facts.shape, 0)
+    note_at = (c * grid.z + z) * grid.y + y
+    first_rows = jnp.where(facts_row < 2, weight, facts_f)
+    notes[note_at] = jnp.concatenate([first_rows, jnp.zeros_like(first_rows)], axis=0).astype(BF)
     here.greet()
+    mine = notes.at[note_at]
+    note_y = exchange(
+        grid.y,
+        y,
+        here.along_y,
+        lambda to: mine,
+        lambda slot: notes.at[(c * grid.z + z) * grid.y + slot],
+        *of("note", "y"),
+    )
+    items = spread_z(here, line, 2, *of("line", "z"))
+    people = spread_x(here, users, per, *of("users", "x"))
+    note_z = spread_z(here, notes, grid.y, *of("note", "z"))
+    next(note_y)
+    next(items)
+    next(people)
     sums[0] = jnp.zeros_like(sums[0])
     for it in range(ITERS):
         near = scratch[f"near{it}"]
         for s in range(grid.c * grid.y):
             near[s * near_rows] = jnp.zeros(near.shape[1:], BF)
-    ends = []
+    next(note_y)
+    next(note_z)
+    unpack_masks(observed, scratch["masks"])
+    next(note_z)
+    next(items)
+    next(note_z)
+    next(note_z)
+    work_out_tables(here, tiles, notes, scratch["serves"], scratch["column_v"], scratch["item_v"])
+    copies = [
+        pltpu.make_async_copy(scratch[f"{name}_v"], scratch[f"{name}_s"], scratch[f"{name}_sem"].at[0])
+        for name in ("column", "item")
+    ]
+    for copy in copies:
+        copy.start()
+    next(items)
+    for copy in copies:
+        copy.wait()
+    tables["column"] = scratch["column_s"]
+    own = c * grid.y + y
+    next(items)
+    next(people)
+    ends += [note_y, items, people, note_z]
     gram_item = None
     for it in range(ITERS):
         sel, query, stage_x, got_x, raw_u, new_users, near, stage, got, fars, got_far, raw_i = (
@@ -417,7 +480,8 @@
 
             @pl.loop(0, tiles)
             def _(t):
-                sel[to * tiles + t] = line[tables["ask"][to * tiles + t]]
+                at = tables["column"][0, (c * grid.y + to) * tiles + t]
+                sel[to * tiles + t] = line[within(at, line)]
 
         asked = exchange(
             grid.y,
@@ -434,9 +498,9 @@
         next(asked)
         ends.append(asked)
         if it == 0:
-            residual_tiles(tables, query, notes, users, ratings, observed, res, res_t)
-
-        @pl.loop(0, tiles)
+            residual_tiles(tables, own, query, notes, users, ratings, scratch["masks"], res, res_t)
+
+        @pl.loop(0, tiles, unroll=4)
         def _(t):
             product = jnp.dot(query[tables["query_at"][t]], res_t[t], preferred_element_type=F32)
             sums[t + 1] = product + sums[tables["user_before"][t]]
@@ -446,7 +510,11 @@
 
             @pl.loop(0, per)
             def _(j):
-                stage_x[to * per + j] = sums[tables["user_last"][to * per + j]]
+                total = sums[tables["user_last"][to * per + j]]
+                if i:
+                    stage_x[to * per + j] = total.astype(BF)
+                else:
+                    raw_u[j] = total
 
         parts = exchange(
             grid.x,
@@ -458,16 +526,16 @@
         )
         next(parts)
         if gram_item is not None:
-            for _ in range(3):
+            for _ in range(2):
                 next(gram_item)
         next(parts)
         ends.append(parts)
 
         @pl.loop(0, per)
         def _(j):
-            total = stage_x[x * per + j]
+            total = raw_u[j]
             for i in range(1, grid.x):
-                total = total + got_x[((x + i) % grid.x) * per + j]
+                total = total + got_x[((x + i) % grid.x) * per + j].astype(F32)
             if it:
                 total = apply_inverse(scratch[f"gitem{it - 1}_work"], total)
             raw_u[j] = total
@@ -481,10 +549,10 @@
         next(gram_user)
         ends.append(people)
 
-        @pl.loop(0, tiles)
+        @pl.loop(0, tiles, unroll=4)
         def _(t):
             product = jnp.dot(new_users[tables["user_at"][t]], res[t], preferred_element_type=F32)
-            total = product + sums[tables["item_before"][t]]
+            total = product + sums[within(tables["column"][2, own * tiles + t], sums)]
             sums[t + 1] = total
             near[(c * grid.y + y) * near_rows + 1 + t] = total.astype(BF)
 
@@ -514,8 +582,8 @@
         def gathered(zz, b):
             total = None
             for s in range(grid.c * grid.y):
-                at = tables["item_table"][(s * grid.z + zz) * 2 + b]
-                value = near[at].astype(F32)
+                at = scratch["item_s"][s, zz * 2 + b]
+                value = near[within(at, near)].astype(F32)
                 total = value if total is None else total + value
             return total
 
@@ -544,7 +612,6 @@
                     stage[starts[way] + len(parts_) * k + j] = gathered(zz, b).astype(BF)
 
             near_z(way).start()
-        next(gram_user)
         for k in range(far):
             for b in range(2):
                 fars[2 * k + b] = gathered(here.z_off(4 * k), b)
@@ -587,7 +654,7 @@
             raw_i[b] = apply_inverse(scratch[f"guser{it}_work"], total)
         gram_item = gram_steps(here, raw_i, 2, counts[1], of("gitem", it))
         if it + 1 < ITERS:
-            line = scratch["line"]
+            line = scratch["next_line"]
             for b in range(2):
                 line[(c * grid.z + z) * 2 + b] = raw_i[b].astype(BF)
             items = spread_z(here, line, 2, *of("zall", it))
@@ -605,7 +672,7 @@
                 user_out[:, j * side : (j + 1) * side] = apply_inverse(
                     scratch[f"guser{it}_work"], raw_u[j]
                 ).astype(BF)
-            for _ in range(6):
+            for _ in range(5):
                 next(gram_item)
             for b in range(2):
                 item_out[:, b * side : (b + 1) * side] = apply_inverse(
@@ -633,12 +700,30 @@
         "res_t": pltpu.VMEM((tiles, side, side), BF),
         "sums": vmem(tiles + 1, F32),
         "line": vmem(2 * grid.z * 2),
+        "next_line": vmem(2 * grid.z * 2),
+        "users": vmem(grid.x * per),
+        "notes": pltpu.VMEM((2 * grid.z * grid.y, 16, side), BF),
+        "masks": pltpu.VMEM((tiles, side, side), BF),
+        "serves": pltpu.VMEM((2 * grid.z * grid.y, side), F32),
+        "column_v": pltpu.VMEM((8, grid.c * grid.y * tiles), jnp.int32),
+        "column_s": pltpu.SMEM((8, grid.c * grid.y * tiles), jnp.int32),
+        "column_sem": sems(1),
+        "item_v": pltpu.VMEM((grid.c * grid.y, side), jnp.int32),
+        "item_s": pltpu.SMEM((grid.c * grid.y, side), jnp.int32),
+        "item_sem": sems(1),
+        "notey_send": sems(grid.y),
+        "notey_recv": sems(grid.y),
+        "usersx_send": sems(grid.x),
+        "usersx_recv": sems(grid.x),
     }
+    for prefix in ("linez", "notez"):
+        for i, shape in enumerate(spread_z_sems(grid)):
+            out[f"{prefix}_{i}"] = shape
     for it in range(ITERS):
         out[f"sel{it}"] = vmem(grid.y * tiles)
         out[f"query{it}"] = vmem(grid.y * tiles)
-        out[f"stage_x{it}"] = vmem(grid.x * per, F32)
-        out[f"got_x{it}"] = vmem(grid.x * per, F32)
+        out[f"stage_x{it}"] = vmem(grid.x * per)
+        out[f"got_x{it}"] = vmem(grid.x * per)
         out[f"raw_u{it}"] = vmem(per, F32)
         out[f"users{it}"] = vmem(grid.x * per)
         out[f"near{it}"] = vmem(grid.c * grid.y * (tiles + 1))
@@ -668,10 +753,10 @@
     return out
 
 
-def main_call(grid, counts, tables, line, notes, users, ratings, observed):
+def main_call(grid, counts, tables, facts, item_start, user_start, ratings, observed):
     tiles, side = ratings.shape[:2]
-    rank = line.shape[1]
-    per = users.shape[0] // grid.x
+    rank = item_start.shape[0]
+    per = user_start.shape[1] // side
     scratch = main_scratch(grid, rank, side, tiles, per)
     return pl.pallas_call(
         functools.partial(main_kernel, grid, counts, tuple(scratch)),
@@ -686,11 +771,7 @@
         compiler_params=pltpu.CompilerParams(
             collective_id=1, has_side_effects=True, vmem_limit_bytes=VMEM_LIMIT
         ),
-    )(*(tables[name] for name in TABLES), line, notes, users, ratings, observed)
-
-
-def to_blocks(factor, side):
-    return jnp.transpose(factor.reshape(factor.shape[0], -1, side), (1, 0, 2))
+    )(*(tables[name] for name in TABLES), facts, item_start, user_start, ratings, observed)
 
 
 def links(ids):
@@ -712,47 +793,17 @@
     owners = grid.y * grid.z * grid.c
     counts = (own_users * owners * grid.x * 1.0, item_start.shape[1] * owners * grid.x * 1.0)
     per = own_users // side
-    r = lax.axis_index("rows")
-    y, z, c = r // (grid.z * grid.c), (r // grid.c) % grid.z, r % grid.c
-
-    weight = ((LEVELS + 1.0) / (exposure.astype(F32) + 1.0)).astype(BF).reshape(2, side)
-    serve = jnp.zeros((1, side), BF).at[0, :owners].set(serve_list.astype(BF))
-    slot = jnp.zeros((1, side), BF).at[0, :tiles].set(tile_slot.astype(BF))
-    note = jnp.concatenate([weight, serve, slot, jnp.zeros((12, side), BF)], 0)
-    line, notes, users = first_gather(grid, to_blocks(item_start, side), note, to_blocks(user_start, side))
-
-    known = notes.reshape(grid.c, grid.z, grid.y, 16, side)[:, :, :, 2:4].astype(jnp.int32)
-    slots = lax.dynamic_index_in_dim(known, z, 1, keepdims=False)[:, :, 1, :tiles]
-    slots = slots.reshape(grid.c * grid.y, tiles)
-    serves = known[:, :, :, 0, :owners].reshape(owners, grid.y, grid.z, grid.c)
-    serves = lax.dynamic_index_in_dim(serves, z, 2, keepdims=False)
-    serves = jnp.transpose(serves, (2, 1, 0)).reshape(grid.c * grid.y, owners)
-    sy, sz, sc = slots // (grid.z * grid.c), (slots // grid.c) % grid.z, slots % grid.c
-    where = (sc * grid.z + sz) * grid.y + sy
-    hit = where[:, :, None] == jnp.arange(owners, dtype=jnp.int32)
-    picks = jnp.sum(jnp.where(hit, serves[:, None, :], 0), axis=2)
-    in_line = (sc * grid.z + sz) * 2 + picks
-    asks = jnp.where(sy == y, in_line, 0).reshape(grid.c, grid.y, tiles)
-    own = c * grid.y + y
-
-    def mine(value):
-        return lax.dynamic_index_in_dim(value, own, 0, keepdims=False)
-
-    note_at, pick = mine(where), mine(picks)
-    last = lasts(jnp.where((sy == y) & (sc == c), sz * 2 + picks, -1), 2 * grid.z)
-    first_row = jnp.arange(grid.c * grid.y, dtype=jnp.int32)[:, None] * (tiles + 1)
+    sy, sz, sc = slots_of(grid, tile_slot)
     tables = {
         "user_at": tile_user,
-        "query_at": mine(sy) * tiles + jnp.arange(tiles, dtype=jnp.int32),
-        "note_at": note_at,
-        "pick": pick,
-        "ask": lax.dynamic_index_in_dim(asks, c, 0, keepdims=False).reshape(-1),
+        "query_at": sy * tiles + jnp.arange(tiles, dtype=jnp.int32),
+        "note_at": (sc * grid.z + sz) * grid.y + sy,
         "user_before": links(tile_user),
         "user_last": lasts(tile_user, grid.x * per),
-        "item_before": links(note_at * 2 + pick),
-        "item_table": (last + first_row).reshape(-1),
     }
-    return main_call(grid, counts, tables, line, notes, users, ratings, observed)
+    rows = [exposure, jnp.pad(serve_list, (0, side - owners)), jnp.pad(tile_slot, (0, side - tiles))]
+    facts = jnp.concatenate(rows + [jnp.zeros((4 * side,), jnp.int32)]).reshape(8, side)
+    return main_call(grid, counts, tables, facts, item_start, user_start, ratings, observed)
 
 
 def solution(mesh):

time: 277 us -> 230 us (0.83)
  Pallas kernels: 253 us -> 222 us
  local copies, waits for them, and re-layouts: 14.5 us -> 6.63 us
  other arithmetic: 6.47 us -> 0.31 us
    pallas_call x1 -> x0, Pallas kernels: 37.4 us -> none  [first_gather(): pl.pallas_call(functools.partial(first_kernel, grid), out_shape=(jax.Shap...]
    pallas_call x1, Pallas kernels: 216 us -> 222 us  [main_call(): pl.pallas_call(functools.partial(main_kernel, grid, counts, tuple(scratch...]
    another operation x1 -> x0, local copies, waits for them, and re-layouts: 3.34 us -> none  [local(): serves = known[:, :, :, 0, :owners].reshape(owners, grid.y, grid.z, grid.c)]
    slice x3 -> x0, local copies, waits for them, and re-layouts: 3.17 us -> none  [the longest x1 3.09 us: local(): serves = known[:, :, :, 0, :owners].reshape(owners, grid.y, grid.z, grid.c)]
    unnamed x13 -> x18, local copies, waits for them, and re-layouts: 6.6 us -> 6.63 us
where the time goes in v3:
time: 230 us
  Pallas kernels  222 us (97%)
  local copies, waits for them, and re-layouts  6.63 us (3%)
    pallas_call x1, Pallas kernels, main_call(): pl.pallas_call(functools.partial(main_kernel, grid, counts, tuple(scratch...  222 us
    unnamed x18, local copies, waits for them, and re-layouts  6.63 us

profile of v3, /device:TPU:1, one launch (start us, length us, event | category | flops | bytes accessed | tf_op | source)
XLA Modules:
  0.0 229.5 jit_solution(7141821679334260752)
XLA Ops:
  0.6 0.0 copy-start.4
  0.6 0.6 copy-done.4
  1.3 0.1 select_reduce_fusion.refs_4_
  1.4 0.0 copy-start.6
  1.4 0.2 select_reduce_fusion.1.refs_3_
  1.6 0.5 copy-done.6
  2.1 0.0 copy-start.5
  2.1 0.0 copy-start.7
  2.1 0.6 copy-done.5
  2.7 0.0 copy-done.7
  2.8 0.0 copy-start
  2.8 1.0 copy-done
  3.8 0.0 copy-start.1
  3.8 0.9 copy-done.1
  4.7 0.0 copy-start.2
  4.7 0.9 copy-done.2
  5.6 0.0 copy-start.3
  5.6 0.8 copy-done.3
  6.4 221.9 %shard_map.95 = (bf16[64,1024]{1,0:T(8,128)(2,1)S(1)}, bf16[64,256]{1,0:T(8,128)(2,1)S(1)}) custom-call(s32[16]{0:T(128)S(1)} %copy-done.4, s32[16]{0:T(128)S(1)} %iota_add_fusion.1.refs_1_, s32[16]{0:T(128)S(1)} %get-tuple-element.2.refs_2_, s32[16]{0:T(128)S(1)} %select_reduce_fusion.1.refs_3_, s32[32]{0:T(128)S(1)} %select_reduce_fusion.refs_4_, ...), custom_call_target="tpu_custom_call" | custom-call | tf_op jit(solution)/shard_map/pallas_call | solution.py:761
  228.2 0.7 copy.12
  228.9 0.6 copy.13
  (5 shorter events, 0.0 us)
Async XLA Ops:
  0.6 0.7 copy-start.4
  1.4 0.7 copy-start.6
  2.1 0.7 copy-start.5
  2.1 0.7 copy-start.7
  2.8 1.0 copy-start
  3.8 0.9 copy-start.1
  4.7 0.9 copy-start.2
  5.6 0.8 copy-start.3

commit v4 on v3

v4 whole, which is shorter than its diff:
```python
import functools

import jax
import jax.numpy as jnp
from jax import lax
from jax.experimental import pallas as pl
from jax.experimental.pallas import tpu as pltpu
from jax.sharding import PartitionSpec as P

LEVELS = 16
ITERS = 2
MESH = pl.DeviceIdType.MESH
BF = jnp.bfloat16
F32 = jnp.float32
HIGHEST = lax.Precision.HIGHEST
VMEM_LIMIT = 48 * 1024 * 1024


class Grid:
    def __init__(self, rows, rep):
        self.c = 2
        self.x = rep
        self.y = 4
        self.z = rows // (self.c * self.y)


class Names:
    def __init__(self, **named):
        self.__dict__.update(named)


def named(tree):
    if isinstance(tree, dict):
        return Names(**{key: named(value) for key, value in tree.items()})
    return [named(value) for value in tree] if isinstance(tree, (list, tuple)) else tree


class Here:
    def __init__(self, grid):
        r = lax.axis_index("rows")
        self.grid = grid
        self.r = r
        self.x = lax.axis_index("rep")
        self.y = r // (grid.z * grid.c)
        self.z = (r // grid.c) % grid.z
        self.c = r % grid.c

    def along_x(self, to):
        return self.r, to

    def along_y(self, to):
        return (to * self.grid.z + self.z) * self.grid.c + self.c, self.x

    def along_z(self, to):
        return (self.y * self.grid.z + to) * self.grid.c + self.c, self.x

    def along_yc(self, to):
        y, c = to // self.grid.c, to % self.grid.c
        return (y * self.grid.z + self.z) * self.grid.c + c, self.x

    def other_core(self):
        return (self.y * self.grid.z + self.z) * self.grid.c + 1 - self.c, self.x

    def z_off(self, by):
        return (self.z + by + 2 * self.grid.z) % self.grid.z

    def greet(self):
        grid = self.grid
        targets = [self.along_x((self.x + i) % grid.x) for i in range(1, grid.x)]
        for i in range(grid.y):
            for j in range(grid.c):
                if i or j:
                    to = ((self.y + i) % grid.y) * grid.c + (self.c + j) % 2
                    targets.append(self.along_yc(to))
        targets += [self.along_z(self.z_off(o)) for o in range(1, grid.z)]
        barrier = pltpu.get_barrier_semaphore()
        for target in targets:
            pl.semaphore_signal(barrier, inc=1, device_id=target, device_id_type=MESH)
        yield
        pl.semaphore_wait(barrier, len(targets))
        yield


def remote(src, dst, send_sem, recv_sem, device):
    return pltpu.make_async_remote_copy(
        src_ref=src,
        dst_ref=dst,
        send_sem=send_sem,
        recv_sem=recv_sem,
        device_id=device,
        device_id_type=MESH,
    )


def sems(*shape):
    return pltpu.SemaphoreType.DMA(shape)


def spread_x(here, buf, per, send, recv):
    n = here.grid.x

    def copy(to, slot):
        block = buf.at[pl.ds(slot * per, per)]
        return remote(block, block, send.at[to], recv.at[slot], here.along_x(to))

    for i in range(1, n):
        copy((here.x + i) % n, here.x).start()
    yield
    for i in range(1, n):
        copy((here.x + i) % n, (here.x + i) % n).wait_recv()
    yield
    for i in range(1, n):
        copy((here.x + i) % n, here.x).wait_send()
    yield


def spread_z_sems(grid):
    far = grid.z // 4
    return [sems(far), sems(far), sems(far, 4), sems(far, 4), sems(1), sems(1)]


def spread_z(here, buf, n, far_send, far_recv, near_send, near_recv, c_send, c_recv):
    grid = here.grid
    half = n // 2
    far = grid.z // 4

    def chunk(core, zz, start=0, count=n):
        return buf.at[pl.ds((core * grid.z + zz) * n + start, count)]

    def far_copy(k):
        block = chunk(here.c, here.z)
        return remote(block, block, far_send.at[k], far_recv.at[k], here.along_z(here.z_off(4 * k)))

    def far_arrival(k):
        block = chunk(here.c, here.z_off(-4 * k))
        return remote(block, block, far_send.at[k], far_recv.at[k], here.along_z(here.z_off(-4 * k)))

    ways = [(1, 0, n), (-1, 0, n), (-2, 0, half), (2, half, half)]

    def near_copy(k, way):
        by, start, count = ways[way]
        block = chunk(here.c, here.z_off(-4 * k), start, count)
        return remote(
            block, block, near_send.at[k, way], near_recv.at[k, way], here.along_z(here.z_off(by))
        )

    def near_arrival(k, way):
        by, start, count = ways[way]
        block = chunk(here.c, here.z_off(-by - 4 * k), start, count)
        return remote(
            block, block, near_send.at[k, way], near_recv.at[k, way], here.along_z(here.z_off(-by))
        )

    for k in range(1, far):
        far_copy(k).start()
    for way in range(4):
        near_copy(0, way).start()
    yield
    for k in range(1, far):
        far_arrival(k).wait_recv()
        for way in range(4):
            near_copy(k, way).start()
    yield
    for k in range(far):
        for way in range(4):
            near_arrival(k, way).wait_recv()
    line = buf.at[pl.ds(here.c * grid.z * n, grid.z * n)]
    swap = remote(line, line, c_send.at[0], c_recv.at[0], here.other_core())
    swap.start()
    yield
    line = buf.at[pl.ds((1 - here.c) * grid.z * n, grid.z * n)]
    remote(line, line, c_send.at[0], c_recv.at[0], here.other_core()).wait_recv()
    yield
    swap.wait_send()
    for k in range(far):
        if k:
            far_copy(k).wait_send()
        for way in range(4):
            near_copy(k, way).wait_send()
    yield


def exchange(n, me, device, put, take, send, recv):
    def copy(to):
        return remote(put(to), take(me), send.at[to], recv.at[me], device(to))

    def arrival(slot):
        return remote(put(slot), take(slot), send.at[slot], recv.at[slot], device(slot))

    for i in range(1, n):
        copy((me + i) % n).start()
    yield
    for i in range(1, n):
        arrival((me + i) % n).wait_recv()
    yield
    for i in range(1, n):
        copy((me + i) % n).wait_send()
    yield


def add_up(ref, n):
    total = ref[0]
    for i in range(1, n):
        total = total + ref[i]
    return total


def gram_scratch(grid, rank):
    shape = (rank // grid.x // 2, 2 * rank)
    counts = [grid.x, grid.y * grid.c, grid.z, grid.x]
    buffers = [pltpu.VMEM((n,) + shape, F32) for n in [grid.x] + counts]
    return buffers + [sems(n) for n in counts for _ in range(2)] + [pltpu.VMEM((rank, 2 * rank), F32)]


def gram_steps(here, block, blocks, row_count, scratch):
    grid = here.grid
    part, first, second, third, whole = scratch[:5]
    pairs = [scratch[5 + 2 * i : 7 + 2 * i] for i in range(4)]
    work = scratch[-1]
    total = None
    for i in range(blocks):
        value = block(i)
        one = lax.dot_general(
            value, value, (((1,), (1,)), ((), ())), precision=HIGHEST, preferred_element_type=F32
        )
        total = one if total is None else total + one
    k = total.shape[0]
    rows = k // grid.x
    low = rows // 2
    for p in range(grid.x):
        part[p] = jnp.concatenate(
            [total[p * rows : p * rows + low], total[p * rows + low : (p + 1) * rows]], axis=1
        )
    x, z = here.x, here.z
    group = here.y * grid.c + here.c
    first[x] = part[x]
    ends = []

    def run(n, me, device, put, ref, pair):
        steps = exchange(n, me, device, put, lambda slot: ref.at[slot], *pair)
        next(steps)
        ends.append(steps)
        return steps

    steps = run(grid.x, x, here.along_x, lambda to: part.at[to], first, pairs[0])
    yield
    next(steps)
    second[group] = add_up(first, grid.x)
    mine = second.at[group]
    steps = run(grid.y * grid.c, group, here.along_yc, lambda to, mine=mine: mine, second, pairs[1])
    yield
    next(steps)
    third[z] = add_up(second, grid.y * grid.c)
    mine = third.at[z]
    steps = run(grid.z, z, here.along_z, lambda to, mine=mine: mine, third, pairs[2])
    yield
    next(steps)
    whole[x] = add_up(third, grid.z)
    mine = whole.at[x]
    steps = run(grid.x, x, here.along_x, lambda to, mine=mine: mine, whole, pairs[3])
    yield
    next(steps)
    row = lax.broadcasted_iota(jnp.int32, (low, k), 0)
    lane = lax.broadcasted_iota(jnp.int32, (low, k), 1)
    for p in range(grid.x):
        for h in range(2):
            at = p * rows + h * low
            unit = jnp.where(row + at == lane, 1.0, 0.0).astype(F32)
            value = whole[p][:, h * k : (h + 1) * k] * (1.0 / row_count)
            work[at : at + low, :] = jnp.concatenate([value, unit], axis=1)
    for steps in ends:
        next(steps)
    yield
    row = lax.broadcasted_iota(jnp.int32, (k, 2 * k), 0)
    lane = lax.broadcasted_iota(jnp.int32, (k, 2 * k), 1)

    eliminate(work)
    value = work[...]
    diagonal = jnp.sum(jnp.where(lane == row, value, 0.0), axis=1, keepdims=True)
    work[...] = value * lax.rsqrt(diagonal)
    yield


def eliminate(work, width=4):
    k = work.shape[0]
    row = lax.broadcasted_iota(jnp.int32, (k, 1), 0)
    lane = lax.broadcasted_iota(jnp.int32, work.shape, 1)

    def lane_sum(value, at):
        return jnp.sum(jnp.where(lane[: value.shape[0]] == at, value, 0.0), axis=1, keepdims=True)

    @pl.loop(0, k // width)
    def _(i):
        at = i * width
        value = work[...]
        rows = [work[pl.ds(at + a, 1), :] for a in range(width)]
        columns = [lane_sum(value, at + a) for a in range(width)]
        block = [[lane_sum(rows[a], at + b) for b in range(width)] for a in range(width)]
        for a in range(width):
            inverse = 1.0 / block[a][a]
            left = columns[a] * inverse
            for b in range(a + 1, width):
                factor = block[a][b] * inverse
                rows[b] = rows[b] - factor * rows[a]
                columns[b] = columns[b] - left * block[a][b]
                for d in range(b, width):
                    block[b][d] = block[b][d] - factor * block[a][d]
            value = value - jnp.where(row > at + a, left, 0.0) * rows[a]
        work[...] = value


def apply_inverse(work, value, first=0):
    k = work.shape[0]
    rows = work[first:, k:] if first else work[: value.shape[0], k : k + value.shape[0]]
    return jnp.dot(rows, value, precision=HIGHEST, preferred_element_type=F32)


def slots_of(grid, value):
    return value // (grid.z * grid.c), (value // grid.c) % grid.z, value % grid.c


def work_out_tables(here, tiles, notes, serves, column_table, item_table):
    grid = here.grid
    group = grid.c * grid.y
    n = group * tiles
    owners = grid.c * grid.z * grid.y
    side = notes.shape[2]

    @pl.loop(0, owners)
    def _(i):
        serves[pl.ds(i, 1), :] = notes[i][2:3].astype(F32)

    row = lax.broadcasted_iota(jnp.int32, (n, side), 0)
    lane = lax.broadcasted_iota(jnp.int32, (n, side), 1)
    tile, member = row % tiles, row // tiles
    asked = []
    for core in range(grid.c):
        for y in range(grid.y):
            line = notes[(core * grid.z + here.z) * grid.y + y][3:4].astype(F32)
            asked.append(jnp.broadcast_to(line, (tiles, side)))
    asked = jnp.concatenate(asked, axis=0)

    def column(value):
        return jnp.sum(value, axis=1, keepdims=True)

    slot = column(jnp.where(lane == tile, asked, 0.0)).astype(jnp.int32)
    sy, sz, sc = slots_of(grid, slot)
    where = (sc * grid.z + sz) * grid.y + sy
    hot = jnp.where(lane == where, 1.0, 0.0).astype(BF)[:, :owners]
    served = jnp.dot(hot, serves[...].astype(BF), preferred_element_type=F32)
    asker = ((member % grid.y) * grid.z + here.z) * grid.c + member // grid.y
    pick = column(jnp.where(lane == asker, served, 0.0)).astype(jnp.int32)
    line_at = (sc * grid.z + sz) * 2 + pick
    ask = jnp.where(sy == here.y, line_at, 0)
    ids = where * 2 + pick
    across = jnp.broadcast_to(ids.astype(F32), (n, side)).T.astype(jnp.int32)[:n]
    square_lane, square_row = lane[:, :n], row[:, :n]
    same = (across == ids) & (square_lane // tiles == square_row // tiles) & (square_lane < square_row)
    before = jnp.max(jnp.where(same, square_lane % tiles + 1, 0).astype(F32), axis=1, keepdims=True)
    columns = jnp.where(
        lane == 0, ask.astype(F32), jnp.where(lane == 1, pick.astype(F32), jnp.where(lane == 2, before, 0.0))
    )
    column_table[...] = columns.T[:8].astype(jnp.int32)
    mine = jnp.where((sy == here.y) & (sc == here.c), sz * 2 + pick, -1)
    number = jnp.where(mine == lane, tile + 1, 0).astype(F32)
    for g in range(group):
        last = jnp.max(number[g * tiles : (g + 1) * tiles], axis=0, keepdims=True)
        item_table[g : g + 1, :] = last.astype(jnp.int32) + g * (tiles + 1)


def within(at, ref):
    return jnp.minimum(jnp.maximum(at, 0), ref.shape[0] - 1)


def unpack_masks(observed, masks):
    side = masks.shape[1]

    @pl.loop(0, masks.shape[0])
    def _(t):
        words = observed[t]
        spread = jnp.broadcast_to(words[:, None, :], (words.shape[0], 8, side)).reshape(side, side)
        shift = lax.broadcasted_iota(jnp.int32, (side, side), 0) % 8
        masks[t] = ((spread >> shift) & 1).astype(F32).T.astype(BF)


def residual_tiles(tables, own, query, notes, users, ratings, masks, out, out_t):
    tiles = ratings.shape[0]

    @pl.loop(0, tiles, unroll=4)
    def _(t):
        meta = notes[tables.note_at[t]].astype(F32)
        line = lax.broadcasted_iota(jnp.int32, meta.shape, 0)
        pick = tables.column[1, own * tiles + t]
        weight = jnp.sum(jnp.where(line == pick, meta, 0.0), axis=0, keepdims=True)
        items = jnp.concatenate([part[tables.query_at[t]] for part in query], axis=0)
        guess = lax.dot_general(
            users[tables.user_at[t]], items, (((0,), (0,)), ((), ())), preferred_element_type=F32
        )
        value = masks[t].astype(F32) * weight * (ratings[t].astype(F32) - guess)
        out[t] = value.astype(BF)
        out_t[t] = value.T.astype(BF)


def main_kernel(grid, counts, tree, *refs):
    refs = list(refs)
    tables = Names()
    tables.user_at, tables.query_at, tables.note_at, tables.user_before, tables.user_last = (
        refs.pop(0) for _ in range(5)
    )
    facts, item_start, user_start, ratings_far, observed_far, user_out, item_out = (refs.pop(0) for _ in range(7))
    scratch = named(jax.tree.unflatten(tree, refs))
    here = Here(grid)
    ratings, observed = scratch.ratings, scratch.observed
    loads = [
        pltpu.make_async_copy(observed_far, observed, scratch.load_sem.at[0]),
        pltpu.make_async_copy(ratings_far, ratings, scratch.load_sem.at[1]),
    ]
    for load in loads:
        load.start()
    tiles, side = ratings.shape[:2]
    per = user_out.shape[1] // side
    rank = user_out.shape[0]
    x, y, z, c = here.x, here.y, here.z, here.c
    half = rank // 2
    res, res_t = scratch.res, scratch.res_t
    near_rows = tiles + 1
    far = grid.z // 4

    line, notes, users = scratch.line, scratch.notes, scratch.users
    ends = []
    greeting = here.greet()
    next(greeting)

    for b in range(2):
        line[(c * grid.z + z) * 2 + b] = item_start[:, b * side : (b + 1) * side]
    for j in range(per):
        users[x * per + j] = user_start[:, j * side : (j + 1) * side]
    facts_f = facts[...].astype(F32)
    weight = (LEVELS + 1.0) / (facts_f + 1.0)
    facts_row = lax.broadcasted_iota(jnp.int32, facts.shape, 0)
    note_at = (c * grid.z + z) * grid.y + y
    first_rows = jnp.where(facts_row < 2, weight, facts_f)
    notes[note_at] = jnp.concatenate([first_rows, jnp.zeros_like(first_rows)], axis=0).astype(BF)
    for h in range(2):
        scratch.sums[h][0] = jnp.zeros((half, side), F32)
        for it in range(ITERS):
            near = scratch.half[it][h].near
            for s in range(grid.c * grid.y):
                near[s * near_rows] = jnp.zeros((half, side), BF)
    for load in loads:
        load.wait()
    unpack_masks(observed, scratch.masks)
    next(greeting)
    mine = notes.at[note_at]
    note_y = exchange(
        grid.y,
        y,
        here.along_y,
        lambda to: mine,
        lambda slot: notes.at[(c * grid.z + z) * grid.y + slot],
        *scratch.note_y,
    )
    items = spread_z(here, line, 2, *scratch.line_z)
    people = spread_x(here, users, per, *scratch.users_x)
    note_z = spread_z(here, notes, grid.y, *scratch.note_z)
    next(note_y)
    next(items)
    next(people)
    next(note_y)
    next(note_z)
    next(note_z)
    next(items)
    next(note_z)
    next(items)
    next(note_z)
    work_out_tables(here, tiles, notes, scratch.serves, scratch.column_v, scratch.item_v)
    copies = [
        pltpu.make_async_copy(scratch.column_v, scratch.column_s, scratch.table_sem.at[0]),
        pltpu.make_async_copy(scratch.item_v, scratch.item_s, scratch.table_sem.at[1]),
    ]
    for copy in copies:
        copy.start()
    for copy in copies:
        copy.wait()
    tables.column = scratch.column_s
    own = c * grid.y + y
    next(items)
    next(people)
    ends += [note_y, items, people, note_z]

    def chain(h):
        rows = slice(h * half, (h + 1) * half)
        sums = scratch.sums[h]
        for it in range(ITERS):
            mine, low = scratch.half[it][h], scratch.half[it][0]
            sel, query, stage_x, got_x, pre_u, raw_u = (
                mine.sel,
                mine.query,
                mine.stage_x,
                mine.got_x,
                mine.pre_u,
                mine.raw_u,
            )
            new_users, near, stage, got, fars, got_far, pre_i, raw_i = (
                mine.users,
                mine.near,
                mine.stage,
                mine.got,
                mine.fars,
                mine.got_far,
                mine.pre_i,
                mine.raw_i,
            )
            for i in range(grid.y):
                to = (y + i) % grid.y

                @pl.loop(0, tiles, unroll=4)
                def _(t):
                    at = tables.column[0, (c * grid.y + to) * tiles + t]
                    if it:
                        block = scratch.lines[h][within(at, line)]
                    else:
                        block = line[within(at, line)][rows]
                    sel[to * tiles + t] = block

            asked = exchange(
                grid.y,
                y,
                here.along_y,
                lambda to, sel=sel: sel.at[pl.ds(to * tiles, tiles)],
                lambda slot, query=query: query.at[pl.ds(slot * tiles, tiles)],
                *mine.ysel,
            )
            next(asked)
            query[pl.ds(y * tiles, tiles)] = sel[pl.ds(y * tiles, tiles)]
            yield
            next(asked)
            ends.append(asked)
            if it == 0:
                yield

            @pl.loop(0, tiles, unroll=4)
            def _(t):
                product = jnp.dot(query[tables.query_at[t]], res_t[t], preferred_element_type=F32)
                sums[t + 1] = product + sums[tables.user_before[t]]

            for i in range(1, grid.x + 1):
                to = (x + i) % grid.x

                @pl.loop(0, per, unroll=4)
                def _(j):
                    total = sums[tables.user_last[to * per + j]]
                    if i < grid.x:
                        stage_x[to * per + j] = total.astype(BF)
                    else:
                        pre_u[j] = total

            parts = exchange(
                grid.x,
                x,
                here.along_x,
                lambda to, stage_x=stage_x: stage_x.at[pl.ds(to * per, per)],
                lambda slot, got_x=got_x: got_x.at[pl.ds(slot * per, per)],
                *mine.xsum,
            )
            next(parts)
            yield
            next(parts)
            ends.append(parts)

            @pl.loop(0, per, unroll=4)
            def _(j):
                total = pre_u[j]
                for i in range(1, grid.x):
                    total = total + got_x[((x + i) % grid.x) * per + j].astype(F32)
                if it:
                    pre_u[j] = total
                    work = scratch.gram_item[it - 1][-1]
                    if h:
                        total = apply_inverse(
                            work, jnp.concatenate([low.pre_u[j], total], axis=0), half
                        )
                    else:
                        total = apply_inverse(work, total)
                raw_u[j] = total
                new_users[x * per + j] = total.astype(BF)

            people = spread_x(here, new_users, per, *mine.xall)
            next(people)
            yield
            next(people)
            ends.append(people)

            @pl.loop(0, tiles, unroll=4)
            def _(t):
                product = jnp.dot(new_users[tables.user_at[t]], res[t], preferred_element_type=F32)
                total = product + sums[within(tables.column[2, own * tiles + t], sums)]
                sums[t + 1] = total
                near[own * near_rows + 1 + t] = total.astype(BF)

            def rows_of(core, slot, near=near):
                return near.at[pl.ds((core * grid.y + slot) * near_rows + 1, tiles)]

            along = exchange(
                grid.y, y, here.along_y, lambda to, f=rows_of: f(c, y), lambda slot, f=rows_of: f(c, slot), *mine.ynear
            )
            next(along)
            c_send, c_recv = mine.cnear

            def c_copy(core, slot):
                block = rows_of(core, slot)
                return remote(block, block, c_send.at[slot], c_recv.at[slot], here.other_core())

            c_copy(c, y).start()
            yield
            next(along)
            ends.append(along)
            for i in range(1, grid.y):
                c_copy(c, (y + i) % grid.y).start()
            yield
            for i in range(grid.y):
                c_copy(1 - c, (y + i) % grid.y).wait_recv()

            def gathered(zz, b):
                total = None
                for s in range(grid.c * grid.y):
                    at = scratch.item_s[s, zz * 2 + b]
                    value = near[within(at, near)].astype(F32)
                    total = value if total is None else total + value
                return total

            z_send, z_recv = mine.znear
            ways = [(1, (0, 1)), (-1, (0, 1)), (-2, (0,)), (2, (1,))]
            starts = [0, 2 * far, 4 * far, 5 * far]

            def near_z(way, arrival=False):
                by, parts_ = ways[way]
                count = len(parts_) * far
                to = here.along_z(here.z_off(-by if arrival else by))
                return remote(
                    stage.at[pl.ds(starts[way], count)],
                    got.at[pl.ds(starts[way], count)],
                    z_send.at[way],
                    z_recv.at[way],
                    to,
                )

            for way in (3, 2, 1, 0):
                by, parts_ = ways[way]

                @pl.loop(0, far)
                def _(k):
                    for j, b in enumerate(parts_):
                        zz = here.z_off(by + 4 * k)
                        stage[starts[way] + len(parts_) * k + j] = gathered(zz, b).astype(BF)

                near_z(way).start()

            @pl.loop(0, far)
            def _(k):
                for b in range(2):
                    fars[2 * k + b] = gathered(here.z_off(4 * k), b)

            yield
            for way in range(4):
                near_z(way, True).wait_recv()
            f_send, f_recv = mine.zfar
            far_stage = mine.far_stage

            def far_copy(k):
                return remote(
                    far_stage.at[pl.ds(2 * k, 2)],
                    got_far.at[pl.ds(2 * k, 2)],
                    f_send.at[k],
                    f_recv.at[k],
                    here.along_z(here.z_off(4 * k)),
                )

            for k in list(range(1, far)) + [0]:
                for b in range(2):
                    total = (
                        fars[2 * k + b]
                        + got[starts[0] + 2 * k + b].astype(F32)
                        + got[starts[1] + 2 * k + b].astype(F32)
                        + got[starts[2 + b] + k].astype(F32)
                    )
                    if k:
                        far_stage[2 * k + b] = total.astype(BF)
                    else:
                        pre_i[b] = total
                if k:
                    far_copy(k).start()
            yield
            for k in range(1, far):
                far_copy(k).wait_recv()
            work = scratch.gram_user[it][-1]
            for b in range(2):
                total = pre_i[b]
                for k in range(1, far):
                    total = total + got_far[2 * k + b].astype(F32)
                pre_i[b] = total
                if h:
                    raw_i[b] = apply_inverse(
                        work, jnp.concatenate([low.pre_i[b], total], axis=0), half
                    )
                else:
                    raw_i[b] = apply_inverse(work, total)
            if it + 1 < ITERS:
                next_line = scratch.lines[h]
                for b in range(2):
                    next_line[(c * grid.z + z) * 2 + b] = raw_i[b].astype(BF)
                items = spread_z(here, next_line, 2, *mine.zall)
                ends.append(items)
                for _ in range(3):
                    next(items)
                    yield
                next(items)
            for i in range(grid.y):
                c_copy(c, (y + i) % grid.y).wait_send()
            for way in range(4):
                near_z(way).wait_send()
            for k in range(1, far):
                far_copy(k).wait_send()
        yield

    def whole_of(low, high):
        return lambda i: jnp.concatenate([low[i], high[i]], axis=0)

    chains = [chain(0), chain(1)]

    def step():
        for one in chains:
            next(one)

    gram_item = None
    for it in range(ITERS):
        if it == 0:
            step()
            step()
            query = [one.query for one in scratch.half[0]]
            residual_tiles(tables, own, query, notes, users, ratings, scratch.masks, res, res_t)
            step()
        else:
            step()
            next(gram_item)
            step()
            next(gram_item)
            next(gram_item)
        step()
        gram_user = gram_steps(here, whole_of(*(one.raw_u for one in scratch.half[it])), per, counts[0], scratch.gram_user[it])
        next(gram_user)
        step()
        next(gram_user)
        step()
        next(gram_user)
        step()
        next(gram_user)
        step()
        next(gram_user)
        next(gram_user)
        step()
        gram_item = gram_steps(here, whole_of(*(one.raw_i for one in scratch.half[it])), 2, counts[1], scratch.gram_item[it])
        next(gram_item)
        if it + 1 < ITERS:
            step()
            next(gram_item)
            step()
            next(gram_item)
    users_of = whole_of(*(one.raw_u for one in scratch.half[-1]))
    items_of = whole_of(*(one.raw_i for one in scratch.half[-1]))
    for j in range(per):
        user_out[:, j * side : (j + 1) * side] = apply_inverse(
            scratch.gram_user[ITERS - 1][-1], users_of(j)
        ).astype(BF)
    for _ in range(5):
        next(gram_item)
    for b in range(2):
        item_out[:, b * side : (b + 1) * side] = apply_inverse(
            scratch.gram_item[ITERS - 1][-1], items_of(b)
        ).astype(BF)
    for steps in ends:
        next(steps)


def main_scratch(grid, rank, side, tiles, per):
    far = grid.z // 4
    asked = grid.c * grid.y * tiles

    def vmem(n, kind=BF, rows=rank // 2):
        return pltpu.VMEM((n, rows, side), kind)

    def pair(n):
        return [sems(n), sems(n)]

    def half():
        return dict(
            sel=vmem(grid.y * tiles),
            query=vmem(grid.y * tiles),
            stage_x=vmem(grid.x * per),
            got_x=vmem(grid.x * per),
            pre_u=vmem(per, F32),
            raw_u=vmem(per, F32),
            users=vmem(grid.x * per),
            near=vmem(grid.c * grid.y * (tiles + 1)),
            stage=vmem(6 * far),
            got=vmem(6 * far),
            fars=vmem(2 * far, F32),
            far_stage=vmem(2 * far),
            got_far=vmem(2 * far),
            pre_i=vmem(2, F32),
            raw_i=vmem(2, F32),
            ysel=pair(grid.y),
            xsum=pair(grid.x),
            xall=pair(grid.x),
            ynear=pair(grid.y),
            cnear=pair(grid.y),
            znear=pair(4),
            zfar=pair(far),
            zall=spread_z_sems(grid),
        )

    return dict(
        ratings=pltpu.VMEM((tiles, side, side), BF),
        observed=pltpu.VMEM((tiles, side // 8, side), jnp.int32),
        load_sem=sems(2),
        res=pltpu.VMEM((tiles, side, side), BF),
        res_t=pltpu.VMEM((tiles, side, side), BF),
        sums=[vmem(tiles + 1, F32) for _ in range(2)],
        line=vmem(2 * grid.z * 2, BF, rank),
        lines=[vmem(2 * grid.z * 2) for _ in range(2)],
        users=vmem(grid.x * per, BF, rank),
        notes=pltpu.VMEM((2 * grid.z * grid.y, 16, side), BF),
        masks=pltpu.VMEM((tiles, side, side), BF),
        serves=pltpu.VMEM((2 * grid.z * grid.y, side), F32),
        column_v=pltpu.VMEM((8, asked), jnp.int32),
        column_s=pltpu.SMEM((8, asked), jnp.int32),
        item_v=pltpu.VMEM((grid.c * grid.y, side), jnp.int32),
        item_s=pltpu.SMEM((grid.c * grid.y, side), jnp.int32),
        table_sem=sems(2),
        note_y=pair(grid.y),
        users_x=pair(grid.x),
        line_z=spread_z_sems(grid),
        note_z=spread_z_sems(grid),
        half=[[half() for _ in range(2)] for _ in range(ITERS)],
        gram_user=[gram_scratch(grid, rank) for _ in range(ITERS)],
        gram_item=[gram_scratch(grid, rank) for _ in range(ITERS)],
    )


def main_call(grid, counts, tables, facts, item_start, user_start, ratings, observed):
    tiles, side = ratings.shape[:2]
    rank = item_start.shape[0]
    per = user_start.shape[1] // side
    scratch, tree = jax.tree.flatten(main_scratch(grid, rank, side, tiles, per))
    return pl.pallas_call(
        functools.partial(main_kernel, grid, counts, tree),
        out_shape=(
            jax.ShapeDtypeStruct((rank, per * side), BF),
            jax.ShapeDtypeStruct((rank, 2 * side), BF),
        ),
        in_specs=[pl.BlockSpec(memory_space=pltpu.SMEM)] * len(tables)
        + [pl.BlockSpec(memory_space=pltpu.VMEM)] * 3
        + [pl.BlockSpec(memory_space=pltpu.HBM)] * 2,
        out_specs=(pl.BlockSpec(memory_space=pltpu.VMEM),) * 2,
        scratch_shapes=scratch,
        compiler_params=pltpu.CompilerParams(
            collective_id=1, has_side_effects=True, vmem_limit_bytes=VMEM_LIMIT
        ),
    )(*tables, facts, item_start, user_start, ratings, observed)


def links(ids):
    at = jnp.arange(ids.shape[0], dtype=jnp.int32)
    same = (ids[:, None] == ids[None, :]) & (at[None, :] < at[:, None])
    return jnp.max(jnp.where(same, at[None, :] + 1, 0), axis=1)


def lasts(ids, n):
    tiles = ids.shape[-1]
    same = ids[..., None, :] == jnp.arange(n, dtype=jnp.int32)[:, None]
    return jnp.max(jnp.where(same, jnp.arange(1, tiles + 1, dtype=jnp.int32), 0), axis=-1)


def local(grid, ratings, observed, user_start, item_start, exposure, serve_list, tile_slot, tile_user):
    side = ratings.shape[2]
    own_users = user_start.shape[1]
    tiles = ratings.shape[0]
    owners = grid.y * grid.z * grid.c
    counts = (own_users * owners * grid.x * 1.0, item_start.shape[1] * owners * grid.x * 1.0)
    per = own_users // side
    sy, sz, sc = slots_of(grid, tile_slot)
    tables = (
        tile_user,
        sy * tiles + jnp.arange(tiles, dtype=jnp.int32),
        (sc * grid.z + sz) * grid.y + sy,
        links(tile_user),
        lasts(tile_user, grid.x * per),
    )
    rows = [exposure, jnp.pad(serve_list, (0, side - owners)), jnp.pad(tile_slot, (0, side - tiles))]
    facts = jnp.concatenate(rows + [jnp.zeros((4 * side,), jnp.int32)]).reshape(8, side)
    return main_call(grid, counts, tables, facts, item_start, user_start, ratings, observed)


def solution(mesh):
    grid = Grid(mesh.shape["rows"], mesh.shape["rep"])
    both = P(("rows", "rep"))
    second = P(None, ("rows", "rep"))
    return jax.shard_map(
        functools.partial(local, grid),
        mesh=mesh,
        in_specs=(both, both, second, second, both, both, both, both),
        out_specs=(second, second),
        check_vma=False,
    )
```

time: 230 us -> 207 us (0.900)
  Pallas kernels: 222 us -> 198 us
    pallas_call x1, Pallas kernels: 222 us -> 198 us  [main_call(): pl.pallas_call(functools.partial(main_kernel, grid, counts, tree), out_sh...]
where the time goes in v4:
time: 207 us; the launch traced here: 206 us
  Pallas kernels  198 us (96%)
  local copies, waits for them, and re-layouts  6.63 us (3%)
    pallas_call x1, Pallas kernels, main_call(): pl.pallas_call(functools.partial(main_kernel, grid, counts, tree), out_sh...  198 us
    unnamed x18, local copies, waits for them, and re-layouts  6.63 us

profile of v4, /device:TPU:1, one launch (start us, length us, event | category | flops | bytes accessed | tf_op | source)
XLA Modules:
  0.0 205.7 jit_solution(8502596240641661383)
XLA Ops:
  0.6 0.0 copy-start.4
  0.6 0.6 copy-done.4
  1.3 0.1 select_reduce_fusion.refs_4_
  1.4 0.0 copy-start.6
  1.4 0.2 select_reduce_fusion.1.refs_3_
  1.6 0.5 copy-done.6
  2.1 0.0 copy-start.5
  2.1 0.0 copy-start.7
  2.1 0.6 copy-done.5
  2.7 0.0 copy-done.7
  2.8 0.0 copy-start
  2.8 1.0 copy-done
  3.8 0.0 copy-start.1
  3.8 0.9 copy-done.1
  4.7 0.0 copy-start.2
  4.7 0.9 copy-done.2
  5.6 0.0 copy-start.3
  5.6 0.8 copy-done.3
  6.4 198.0 %shard_map.95 = (bf16[64,1024]{1,0:T(8,128)(2,1)S(1)}, bf16[64,256]{1,0:T(8,128)(2,1)S(1)}) custom-call(s32[16]{0:T(128)S(1)} %copy-done.4, s32[16]{0:T(128)S(1)} %iota_add_fusion.1.refs_1_, s32[16]{0:T(128)S(1)} %get-tuple-element.2.refs_2_, s32[16]{0:T(128)S(1)} %select_reduce_fusion.1.refs_3_, s32[32]{0:T(128)S(1)} %select_reduce_fusion.refs_4_, ...), custom_call_target="tpu_custom_call" | custom-call | tf_op jit(solution)/shard_map/pallas_call | solution.py:855
  204.4 0.7 copy.12
  205.1 0.6 copy.13
  (5 shorter events, 0.0 us)
Async XLA Ops:
  0.6 0.7 copy-start.4
  1.4 0.7 copy-start.6
  2.1 0.7 copy-start.5
  2.1 0.7 copy-start.7
  2.8 1.0 copy-start
  3.8 0.9 copy-start.1
  4.7 0.9 copy-start.2
  5.6 0.8 copy-start.3

commit v5 on v4

--- a/solution.py
+++ b/solution.py
@@ -13,7 +13,7 @@
 BF = jnp.bfloat16
 F32 = jnp.float32
 HIGHEST = lax.Precision.HIGHEST
-VMEM_LIMIT = 48 * 1024 * 1024
+VMEM_LIMIT = 62 * 1024 * 1024
 
 
 class Grid:
@@ -212,7 +212,7 @@
     return buffers + [sems(n) for n in counts for _ in range(2)] + [pltpu.VMEM((rank, 2 * rank), F32)]
 
 
-def gram_steps(here, block, blocks, row_count, scratch):
+def gram_steps(here, block, blocks, row_count, scratch, scale_only=False):
     grid = here.grid
     part, first, second, third, whole = scratch[:5]
     pairs = [scratch[5 + 2 * i : 7 + 2 * i] for i in range(4)]
@@ -274,10 +274,11 @@
     row = lax.broadcasted_iota(jnp.int32, (k, 2 * k), 0)
     lane = lax.broadcasted_iota(jnp.int32, (k, 2 * k), 1)
 
-    eliminate(work)
+    if not scale_only:
+        eliminate(work)
     value = work[...]
     diagonal = jnp.sum(jnp.where(lane == row, value, 0.0), axis=1, keepdims=True)
-    work[...] = value * lax.rsqrt(diagonal)
+    work[...] = (jnp.ones_like(value) if scale_only else value) * lax.rsqrt(diagonal)
     yield
 
 
@@ -372,6 +373,18 @@
     return jnp.minimum(jnp.maximum(at, 0), ref.shape[0] - 1)
 
 
+def work_out_users(tiles, x_notes, user_table):
+    side = x_notes.shape[2]
+    row = lax.broadcasted_iota(jnp.int32, (tiles, side), 0)
+    lane = lax.broadcasted_iota(jnp.int32, (tiles, side), 1)
+    for x in range(x_notes.shape[0]):
+        line = jnp.broadcast_to(x_notes[x][4:5].astype(F32), (tiles, side))
+        block = jnp.sum(jnp.where(lane == row, line, 0.0), axis=1, keepdims=True).astype(jnp.int32)
+        number = jnp.where(block == lane, row + 1, 0).astype(F32)
+        last = jnp.max(number, axis=0, keepdims=True).astype(jnp.int32)
+        user_table[x : x + 1, :] = last + x * (tiles + 1)
+
+
 def unpack_masks(observed, masks):
     side = masks.shape[1]
 
@@ -404,16 +417,19 @@
 def main_kernel(grid, counts, tree, *refs):
     refs = list(refs)
     tables = Names()
-    tables.user_at, tables.query_at, tables.note_at, tables.user_before, tables.user_last = (
-        refs.pop(0) for _ in range(5)
-    )
-    facts, item_start, user_start, ratings_far, observed_far, user_out, item_out = (refs.pop(0) for _ in range(7))
+    tables.user_at, tables.query_at, tables.note_at, tables.user_before = (refs.pop(0) for _ in range(4))
+    facts, *given, user_out, item_out = (refs.pop(0) for _ in range(7))
     scratch = named(jax.tree.unflatten(tree, refs))
     here = Here(grid)
-    ratings, observed = scratch.ratings, scratch.observed
+    item_start, user_start, ratings, observed = kept = (
+        scratch.item_start,
+        scratch.user_start,
+        scratch.ratings,
+        scratch.observed,
+    )
     loads = [
-        pltpu.make_async_copy(observed_far, observed, scratch.load_sem.at[0]),
-        pltpu.make_async_copy(ratings_far, ratings, scratch.load_sem.at[1]),
+        pltpu.make_async_copy(there, ref, scratch.load_sem.at[i])
+        for i, (there, ref) in enumerate(zip(given, kept))
     ]
     for load in loads:
         load.start()
@@ -431,6 +447,8 @@
     greeting = here.greet()
     next(greeting)
 
+    for load in loads[:2]:
+        load.wait()
     for b in range(2):
         line[(c * grid.z + z) * 2 + b] = item_start[:, b * side : (b + 1) * side]
     for j in range(per):
@@ -447,7 +465,10 @@
             near = scratch.half[it][h].near
             for s in range(grid.c * grid.y):
                 near[s * near_rows] = jnp.zeros((half, side), BF)
-    for load in loads:
+            for s in range(grid.x):
+                scratch.half[it][h].got_x[s * near_rows] = jnp.zeros((half, side), BF)
+    scratch.x_notes[x] = notes[note_at]
+    for load in loads[2:]:
         load.wait()
     unpack_masks(observed, scratch.masks)
     next(greeting)
@@ -460,11 +481,15 @@
         lambda slot: notes.at[(c * grid.z + z) * grid.y + slot],
         *scratch.note_y,
     )
+    note_x = exchange(
+        grid.x, x, here.along_x, lambda to: mine, lambda slot: scratch.x_notes.at[slot], *scratch.note_x
+    )
     items = spread_z(here, line, 2, *scratch.line_z)
     people = spread_x(here, users, per, *scratch.users_x)
     note_z = spread_z(here, notes, grid.y, *scratch.note_z)
     next(note_y)
     next(items)
+    next(note_x)
     next(people)
     next(note_y)
     next(note_z)
@@ -473,10 +498,13 @@
     next(note_z)
     next(items)
     next(note_z)
+    next(note_x)
+    work_out_users(tiles, scratch.x_notes, scratch.user_v)
     work_out_tables(here, tiles, notes, scratch.serves, scratch.column_v, scratch.item_v)
     copies = [
         pltpu.make_async_copy(scratch.column_v, scratch.column_s, scratch.table_sem.at[0]),
         pltpu.make_async_copy(scratch.item_v, scratch.item_s, scratch.table_sem.at[1]),
+        pltpu.make_async_copy(scratch.user_v, scratch.user_s, scratch.table_sem.at[2]),
     ]
     for copy in copies:
         copy.start()
@@ -486,21 +514,14 @@
     own = c * grid.y + y
     next(items)
     next(people)
-    ends += [note_y, items, people, note_z]
+    ends += [note_x, note_y, items, people, note_z]
 
     def chain(h):
         rows = slice(h * half, (h + 1) * half)
         sums = scratch.sums[h]
         for it in range(ITERS):
             mine, low = scratch.half[it][h], scratch.half[it][0]
-            sel, query, stage_x, got_x, pre_u, raw_u = (
-                mine.sel,
-                mine.query,
-                mine.stage_x,
-                mine.got_x,
-                mine.pre_u,
-                mine.raw_u,
-            )
+            sel, query, got_x, raw_u = mine.sel, mine.query, mine.got_x, mine.raw_u
             new_users, near, stage, got, fars, got_far, pre_i, raw_i = (
                 mine.users,
                 mine.near,
@@ -542,54 +563,37 @@
             @pl.loop(0, tiles, unroll=4)
             def _(t):
                 product = jnp.dot(query[tables.query_at[t]], res_t[t], preferred_element_type=F32)
-                sums[t + 1] = product + sums[tables.user_before[t]]
-
-            for i in range(1, grid.x + 1):
-                to = (x + i) % grid.x
-
-                @pl.loop(0, per, unroll=4)
-                def _(j):
-                    total = sums[tables.user_last[to * per + j]]
-                    if i < grid.x:
-                        stage_x[to * per + j] = total.astype(BF)
-                    else:
-                        pre_u[j] = total
+                total = product + sums[tables.user_before[t]]
+                sums[t + 1] = total
+                got_x[x * near_rows + 1 + t] = total.astype(BF)
+
+            def sums_from(slot, got_x=got_x):
+                return got_x.at[pl.ds(slot * near_rows + 1, tiles)]
 
             parts = exchange(
-                grid.x,
-                x,
-                here.along_x,
-                lambda to, stage_x=stage_x: stage_x.at[pl.ds(to * per, per)],
-                lambda slot, got_x=got_x: got_x.at[pl.ds(slot * per, per)],
-                *mine.xsum,
+                grid.x, x, here.along_x, lambda to, f=sums_from: f(x), lambda slot, f=sums_from: f(slot), *mine.xsum
             )
             next(parts)
             yield
             next(parts)
             ends.append(parts)
 
+            def user_sum(block):
+                total = None
+                for s in range(grid.x):
+                    value = got_x[within(scratch.user_s[s, block], got_x)].astype(F32)
+                    total = value if total is None else total + value
+                return total * scratch.gram_item[it - 1][-1][rows] if it else total
+
+            @pl.loop(0, grid.x * per, unroll=4)
+            def _(j):
+                new_users[j] = user_sum(j).astype(BF)
+
             @pl.loop(0, per, unroll=4)
             def _(j):
-                total = pre_u[j]
-                for i in range(1, grid.x):
-                    total = total + got_x[((x + i) % grid.x) * per + j].astype(F32)
-                if it:
-                    pre_u[j] = total
-                    work = scratch.gram_item[it - 1][-1]
-                    if h:
-                        total = apply_inverse(
-                            work, jnp.concatenate([low.pre_u[j], total], axis=0), half
-                        )
-                    else:
-                        total = apply_inverse(work, total)
-                raw_u[j] = total
-                new_users[x * per + j] = total.astype(BF)
-
-            people = spread_x(here, new_users, per, *mine.xall)
-            next(people)
+                raw_u[j] = user_sum(x * per + j)
+
             yield
-            next(people)
-            ends.append(people)
 
             @pl.loop(0, tiles, unroll=4)
             def _(t):
@@ -759,7 +763,14 @@
         next(gram_user)
         next(gram_user)
         step()
-        gram_item = gram_steps(here, whole_of(*(one.raw_i for one in scratch.half[it])), 2, counts[1], scratch.gram_item[it])
+        gram_item = gram_steps(
+            here,
+            whole_of(*(one.raw_i for one in scratch.half[it])),
+            2,
+            counts[1],
+            scratch.gram_item[it],
+            scale_only=it + 1 < ITERS,
+        )
         next(gram_item)
         if it + 1 < ITERS:
             step()
@@ -796,9 +807,7 @@
         return dict(
             sel=vmem(grid.y * tiles),
             query=vmem(grid.y * tiles),
-            stage_x=vmem(grid.x * per),
-            got_x=vmem(grid.x * per),
-            pre_u=vmem(per, F32),
+            got_x=vmem(grid.x * (tiles + 1)),
             raw_u=vmem(per, F32),
             users=vmem(grid.x * per),
             near=vmem(grid.c * grid.y * (tiles + 1)),
@@ -811,7 +820,6 @@
             raw_i=vmem(2, F32),
             ysel=pair(grid.y),
             xsum=pair(grid.x),
-            xall=pair(grid.x),
             ynear=pair(grid.y),
             cnear=pair(grid.y),
             znear=pair(4),
@@ -822,7 +830,13 @@
     return dict(
         ratings=pltpu.VMEM((tiles, side, side), BF),
         observed=pltpu.VMEM((tiles, side // 8, side), jnp.int32),
-        load_sem=sems(2),
+        item_start=pltpu.VMEM((rank, 2 * side), BF),
+        user_start=pltpu.VMEM((rank, per * side), BF),
+        load_sem=sems(4),
+        x_notes=pltpu.VMEM((grid.x, 16, side), BF),
+        user_v=pltpu.VMEM((grid.x, side), jnp.int32),
+        user_s=pltpu.SMEM((grid.x, side), jnp.int32),
+        note_x=pair(grid.x),
         res=pltpu.VMEM((tiles, side, side), BF),
         res_t=pltpu.VMEM((tiles, side, side), BF),
         sums=[vmem(tiles + 1, F32) for _ in range(2)],
@@ -836,7 +850,7 @@
         column_s=pltpu.SMEM((8, asked), jnp.int32),
         item_v=pltpu.VMEM((grid.c * grid.y, side), jnp.int32),
         item_s=pltpu.SMEM((grid.c * grid.y, side), jnp.int32),
-        table_sem=sems(2),
+        table_sem=sems(3),
         note_y=pair(grid.y),
         users_x=pair(grid.x),
         line_z=spread_z_sems(grid),
@@ -859,8 +873,8 @@
             jax.ShapeDtypeStruct((rank, 2 * side), BF),
         ),
         in_specs=[pl.BlockSpec(memory_space=pltpu.SMEM)] * len(tables)
-        + [pl.BlockSpec(memory_space=pltpu.VMEM)] * 3
-        + [pl.BlockSpec(memory_space=pltpu.HBM)] * 2,
+        + [pl.BlockSpec(memory_space=pltpu.VMEM)]
+        + [pl.BlockSpec(memory_space=pltpu.HBM)] * 4,
         out_specs=(pl.BlockSpec(memory_space=pltpu.VMEM),) * 2,
         scratch_shapes=scratch,
         compiler_params=pltpu.CompilerParams(
@@ -873,12 +887,6 @@
     at = jnp.arange(ids.shape[0], dtype=jnp.int32)
     same = (ids[:, None] == ids[None, :]) & (at[None, :] < at[:, None])
     return jnp.max(jnp.where(same, at[None, :] + 1, 0), axis=1)
-
-
-def lasts(ids, n):
-    tiles = ids.shape[-1]
-    same = ids[..., None, :] == jnp.arange(n, dtype=jnp.int32)[:, None]
-    return jnp.max(jnp.where(same, jnp.arange(1, tiles + 1, dtype=jnp.int32), 0), axis=-1)
 
 
 def local(grid, ratings, observed, user_start, item_start, exposure, serve_list, tile_slot, tile_user):
@@ -894,10 +902,9 @@
         sy * tiles + jnp.arange(tiles, dtype=jnp.int32),
         (sc * grid.z + sz) * grid.y + sy,
         links(tile_user),
-        lasts(tile_user, grid.x * per),
     )
-    rows = [exposure, jnp.pad(serve_list, (0, side - owners)), jnp.pad(tile_slot, (0, side - tiles))]
-    facts = jnp.concatenate(rows + [jnp.zeros((4 * side,), jnp.int32)]).reshape(8, side)
+    rows = [exposure] + [jnp.pad(value, (0, side - value.shape[0])) for value in (serve_list, tile_slot, tile_user)]
+    facts = jnp.concatenate(rows + [jnp.zeros((3 * side,), jnp.int32)]).reshape(8, side)
     return main_call(grid, counts, tables, facts, item_start, user_start, ratings, observed)
 
 

time: 207 us -> 213 us (1.029)
  Pallas kernels: 198 us -> 206 us
    pallas_call x1, Pallas kernels: 198 us -> 206 us  [main_call(): pl.pallas_call(functools.partial(main_kernel, grid, counts, tree), out_sh...]
where the time goes in v5:
time: 213 us
  Pallas kernels  206 us (97%)
  local copies, waits for them, and re-layouts  4.78 us (2%)
    pallas_call x1, Pallas kernels, main_call(): pl.pallas_call(functools.partial(main_kernel, grid, counts, tree), out_sh...  206 us
    unnamed x18, local copies, waits for them, and re-layouts  4.78 us

profile of v5, /device:TPU:1, one launch (start us, length us, event | category | flops | bytes accessed | tf_op | source)
XLA Modules:
  0.0 212.9 jit_solution(10199604343679430116)
XLA Ops:
  0.6 0.0 copy-start.1
  0.7 0.6 copy-done.1
  1.3 0.0 copy-start.5
  1.3 0.7 select_reduce_fusion.refs_3_
  2.0 0.0 copy-done.5
  2.0 0.5 multiply_add_fusion
  2.5 0.6 iota_add_fusion.1.refs_1_
  3.1 0.0 copy-start.3
  3.1 0.7 copy-done.3
  3.8 0.0 copy-start.4
  3.8 0.6 copy-done.4
  4.5 0.0 copy-start.2
  4.5 0.6 copy-done.2
  5.1 205.6 %shard_map.95 = (bf16[64,1024]{1,0:T(8,128)(2,1)}, bf16[64,256]{1,0:T(8,128)(2,1)}) custom-call(s32[16]{0:T(128)} %refs_0_.1, s32[16]{0:T(128)} %iota_add_fusion.1.refs_1_, s32[16]{0:T(128)} %get-tuple-element.2.refs_2_, s32[16]{0:T(128)} %select_reduce_fusion.refs_3_, s32[8,128]{1,0:T(8,128)} %bitcast.1, bf16[64,256]{1,0:T(8,128)(2,1)} %refs_5_.1, ...), custom_call_target="tpu_custom_call" | custom-call | tf_op jit(solution)/shard_map/pallas_call | solution.py:869
  210.7 0.0 copy-start
  210.7 1.6 copy.17
  212.3 0.0 copy-done
  212.3 0.6 copy.18
  (7 shorter events, 0.0 us)
Async XLA Ops:
  0.6 0.7 copy-start.1
  1.3 0.7 copy-start.5
  3.1 0.7 copy-start.3
  3.8 0.7 copy-start.4
  4.5 0.6 copy-start.2
  210.7 1.6 copy-start

commit v6 on v4

--- a/solution.py
+++ b/solution.py
@@ -103,7 +103,7 @@
         block = buf.at[pl.ds(slot * per, per)]
         return remote(block, block, send.at[to], recv.at[slot], here.along_x(to))
 
-    for i in range(1, n):
+    for i in sorted(range(1, n), key=lambda i: -min(i, n - i)):
         copy((here.x + i) % n, here.x).start()
     yield
     for i in range(1, n):
@@ -151,14 +151,14 @@
             block, block, near_send.at[k, way], near_recv.at[k, way], here.along_z(here.z_off(-by))
         )
 
-    for k in range(1, far):
+    for k in sorted(range(1, far), key=lambda k: -min(k, far - k)):
         far_copy(k).start()
-    for way in range(4):
+    for way in (2, 3, 0, 1):
         near_copy(0, way).start()
     yield
     for k in range(1, far):
         far_arrival(k).wait_recv()
-        for way in range(4):
+        for way in (2, 3, 0, 1):
             near_copy(k, way).start()
     yield
     for k in range(far):
@@ -187,7 +187,7 @@
     def arrival(slot):
         return remote(put(slot), take(slot), send.at[slot], recv.at[slot], device(slot))
 
-    for i in range(1, n):
+    for i in sorted(range(1, n), key=lambda i: -min(i, n - i)):
         copy((me + i) % n).start()
     yield
     for i in range(1, n):
@@ -386,7 +386,7 @@
 def residual_tiles(tables, own, query, notes, users, ratings, masks, out, out_t):
     tiles = ratings.shape[0]
 
-    @pl.loop(0, tiles, unroll=4)
+    @pl.loop(0, tiles, unroll=8)
     def _(t):
         meta = notes[tables.note_at[t]].astype(F32)
         line = lax.broadcasted_iota(jnp.int32, meta.shape, 0)
@@ -514,7 +514,7 @@
             for i in range(grid.y):
                 to = (y + i) % grid.y
 
-                @pl.loop(0, tiles, unroll=4)
+                @pl.loop(0, tiles, unroll=8)
                 def _(t):
                     at = tables.column[0, (c * grid.y + to) * tiles + t]
                     if it:
@@ -539,7 +539,7 @@
             if it == 0:
                 yield
 
-            @pl.loop(0, tiles, unroll=4)
+            @pl.loop(0, tiles, unroll=8)
             def _(t):
                 product = jnp.dot(query[tables.query_at[t]], res_t[t], preferred_element_type=F32)
                 sums[t + 1] = product + sums[tables.user_before[t]]
@@ -591,7 +591,7 @@
             next(people)
             ends.append(people)
 
-            @pl.loop(0, tiles, unroll=4)
+            @pl.loop(0, tiles, unroll=8)
             def _(t):
                 product = jnp.dot(new_users[tables.user_at[t]], res[t], preferred_element_type=F32)
                 total = product + sums[within(tables.column[2, own * tiles + t], sums)]
@@ -676,7 +676,7 @@
                     here.along_z(here.z_off(4 * k)),
                 )
 
-            for k in list(range(1, far)) + [0]:
+            for k in sorted(range(1, far), key=lambda k: -min(k, far - k)) + [0]:
                 for b in range(2):
                     total = (
                         fars[2 * k + b]

time: 207 us -> 202 us (0.976)
  Pallas kernels: 198 us -> 194 us
    pallas_call x1, Pallas kernels: 198 us -> 194 us  [main_call(): pl.pallas_call(functools.partial(main_kernel, grid, counts, tree), out_sh...]
where the time goes in v6:
time: 202 us
  Pallas kernels  194 us (96%)
  local copies, waits for them, and re-layouts  6.63 us (3%)
    pallas_call x1, Pallas kernels, main_call(): pl.pallas_call(functools.partial(main_kernel, grid, counts, tree), out_sh...  194 us
    unnamed x18, local copies, waits for them, and re-layouts  6.63 us

profile of v6, /device:TPU:1, one launch (start us, length us, event | category | flops | bytes accessed | tf_op | source)
XLA Modules:
  0.0 201.8 jit_solution(11336211161622366594)
XLA Ops:
  0.6 0.0 copy-start.4
  0.6 0.6 copy-done.4
  1.3 0.1 select_reduce_fusion.refs_4_
  1.4 0.0 copy-start.6
  1.4 0.2 select_reduce_fusion.1.refs_3_
  1.6 0.5 copy-done.6
  2.1 0.0 copy-start.5
  2.1 0.0 copy-start.7
  2.1 0.6 copy-done.5
  2.7 0.0 copy-done.7
  2.8 0.0 copy-start
  2.8 1.0 copy-done
  3.8 0.0 copy-start.1
  3.8 0.9 copy-done.1
  4.7 0.0 copy-start.2
  4.7 0.9 copy-done.2
  5.6 0.0 copy-start.3
  5.6 0.8 copy-done.3
  6.4 194.2 %shard_map.95 = (bf16[64,1024]{1,0:T(8,128)(2,1)S(1)}, bf16[64,256]{1,0:T(8,128)(2,1)S(1)}) custom-call(s32[16]{0:T(128)S(1)} %copy-done.4, s32[16]{0:T(128)S(1)} %iota_add_fusion.1.refs_1_, s32[16]{0:T(128)S(1)} %get-tuple-element.2.refs_2_, s32[16]{0:T(128)S(1)} %select_reduce_fusion.1.refs_3_, s32[32]{0:T(128)S(1)} %select_reduce_fusion.refs_4_, ...), custom_call_target="tpu_custom_call" | custom-call | tf_op jit(solution)/shard_map/pallas_call | solution.py:855
  200.6 0.7 copy.12
  201.2 0.6 copy.13
  (5 shorter events, 0.0 us)
Async XLA Ops:
  0.6 0.7 copy-start.4
  1.4 0.7 copy-start.6
  2.1 0.7 copy-start.5
  2.1 0.7 copy-start.7
  2.8 1.0 copy-start
  3.8 0.9 copy-start.1
  4.7 0.9 copy-start.2
  5.6 0.8 copy-start.3

commit v7 on v6

--- a/solution.py
+++ b/solution.py
@@ -180,7 +180,7 @@
     yield
 
 
-def exchange(n, me, device, put, take, send, recv):
+def exchange(n, me, device, put, take, send, recv, prepare=None):
     def copy(to):
         return remote(put(to), take(me), send.at[to], recv.at[me], device(to))
 
@@ -188,6 +188,8 @@
         return remote(put(slot), take(slot), send.at[slot], recv.at[slot], device(slot))
 
     for i in sorted(range(1, n), key=lambda i: -min(i, n - i)):
+        if prepare is not None:
+            prepare((me + i) % n)
         copy((me + i) % n).start()
     yield
     for i in range(1, n):
@@ -511,9 +513,7 @@
                 mine.pre_i,
                 mine.raw_i,
             )
-            for i in range(grid.y):
-                to = (y + i) % grid.y
-
+            def select(to, sel=sel):
                 @pl.loop(0, tiles, unroll=8)
                 def _(t):
                     at = tables.column[0, (c * grid.y + to) * tiles + t]
@@ -530,8 +530,10 @@
                 lambda to, sel=sel: sel.at[pl.ds(to * tiles, tiles)],
                 lambda slot, query=query: query.at[pl.ds(slot * tiles, tiles)],
                 *mine.ysel,
+                prepare=select,
             )
             next(asked)
+            select(y)
             query[pl.ds(y * tiles, tiles)] = sel[pl.ds(y * tiles, tiles)]
             yield
             next(asked)

time: 202 us -> 203 us (level)
  no operation moved by 1% of the time
where the time goes in v7:
time: 203 us; the launch traced here: 202 us
  Pallas kernels  194 us (96%)
  local copies, waits for them, and re-layouts  6.63 us (3%)
    pallas_call x1, Pallas kernels, main_call(): pl.pallas_call(functools.partial(main_kernel, grid, counts, tree), out_sh...  194 us
    unnamed x18, local copies, waits for them, and re-layouts  6.63 us

profile of v7, /device:TPU:1, one launch (start us, length us, event | category | flops | bytes accessed | tf_op | source)
XLA Modules:
  0.0 201.8 jit_solution(8179517930722791412)
XLA Ops:
  0.6 0.0 copy-start.4
  0.6 0.6 copy-done.4
  1.3 0.1 select_reduce_fusion.refs_4_
  1.4 0.0 copy-start.6
  1.4 0.2 select_reduce_fusion.1.refs_3_
  1.6 0.5 copy-done.6
  2.1 0.0 copy-start.5
  2.1 0.0 copy-start.7
  2.1 0.6 copy-done.5
  2.7 0.0 copy-done.7
  2.8 0.0 copy-start
  2.8 1.0 copy-done
  3.8 0.0 copy-start.1
  3.8 0.9 copy-done.1
  4.7 0.0 copy-start.2
  4.7 0.9 copy-done.2
  5.6 0.0 copy-start.3
  5.6 0.8 copy-done.3
  6.4 194.2 %shard_map.95 = (bf16[64,1024]{1,0:T(8,128)(2,1)S(1)}, bf16[64,256]{1,0:T(8,128)(2,1)S(1)}) custom-call(s32[16]{0:T(128)S(1)} %copy-done.4, s32[16]{0:T(128)S(1)} %iota_add_fusion.1.refs_1_, s32[16]{0:T(128)S(1)} %get-tuple-element.2.refs_2_, s32[16]{0:T(128)S(1)} %select_reduce_fusion.1.refs_3_, s32[32]{0:T(128)S(1)} %select_reduce_fusion.refs_4_, ...), custom_call_target="tpu_custom_call" | custom-call | tf_op jit(solution)/shard_map/pallas_call | solution.py:857
  200.5 0.7 copy.12
  201.2 0.6 copy.13
  (5 shorter events, 0.0 us)
Async XLA Ops:
  0.6 0.7 copy-start.4
  1.4 0.7 copy-start.6
  2.1 0.7 copy-start.5
  2.1 0.7 copy-start.7
  2.8 1.0 copy-start
  3.8 0.9 copy-start.1
  4.7 0.9 copy-start.2
  5.6 0.8 copy-start.3
